TPU v7x, 512 devices: a whole 4x8x8 slice. The times are simulated.
512 devices in a mesh: grid: 64 (over x, y_lo, z), member: 8 (over y_hi, core).
Axes of the slice: x: 4, y: 8 (y_hi: 4, y_lo: 2; y = y_hi * 2 + y_lo), z: 8, core: 2. Of those that a mesh axis runs over, the one named last changes fastest.
Arguments:
- fields: bfloat16 [8, 65536, 1024], P('member', 'grid'), may hold values from -0.796875 to 0.796875
- observed: bfloat16 [100, 65536], P(None, 'grid'), may hold values from -6 to 6
- lat_weight: float32 [65536], P('grid'), may hold values from 0.3 to 6, as said below
- var_weight: float32 [100], replicated, may hold values from 0.25 to 4
- weight: bfloat16 [100, 1024], replicated, may hold values from -0.1875 to 0.1875
- bias: float32 [100], replicated, may hold values from -1 to 1
- gain: float32 [1024], replicated, may hold values from 0.1 to 1.9
Outputs:
- grad_fields: bfloat16 [8, 65536, 1024], P('member', 'grid')
- grad_weight: float32 [100, 1024], replicated
- grad_gain: float32 [1024], replicated
- grad_bias: float32 [100], replicated
- loss: float32 [], replicated
Inputs may be any that keep to these rules, and one draw needn't show every extreme that they name: `lat_weight`: positive.
All inputs are finite; a program needn't handle non-finite values.
Results may differ from a plain program's by a relative error of at most 0.0014.
The roundings to bfloat16 on the way count: a program that leaves them out, or rounds other values in their place, can miss the bound.
Values sent between devices are 32-bit elements; how exact they have to be, the bound alone decides.
No kernel may reach another device: no remote copies, remote signals or barrier semaphores. Data moves between devices by JAX's collectives and lax.ppermute only.
A program may use at most 64 MiB of HBM per device.

v0:
```python
import jax
import jax.numpy as jnp
import numpy as np
from jax import lax
from jax.sharding import PartitionSpec as P

soft_square = 0.01
norm_epsilon = 1e-05


def normalize(member_rows, gain):
    values = member_rows.astype(jnp.float32)
    row_mean = jnp.mean(values, axis=-1, keepdims=True)
    centred = values - row_mean
    inv_std = lax.rsqrt(jnp.mean(centred * centred, axis=-1, keepdims=True) + norm_epsilon)
    unit_rows = centred * inv_std
    normed = (unit_rows * gain[None, None, :]).astype(jnp.bfloat16)
    return (normed, unit_rows, inv_std)


def shards(fields, observed, lat_weight, var_weight, weight, bias, gain):
    own_rows = fields.shape[0]
    local_points = fields.shape[1]
    members = own_rows * lax.axis_size("member")
    normed, unit_rows, inv_std = normalize(fields, gain)
    predicted = (
        jnp.einsum("vd,rpd->rvp", weight, normed, preferred_element_type=jnp.float32)
        + bias[None, :, None]
    )
    lat_total = lax.psum(jnp.sum(lat_weight), "grid")
    target = observed.astype(jnp.float32)
    obs_gap = predicted - target[None]
    obs_abs = jnp.sqrt(obs_gap * obs_gap + soft_square)
    obs_sign = obs_gap / obs_abs
    weight_grid = var_weight[:, None] * lat_weight[None, :]
    scale_pair = 1.0 / (members * (members - 1))
    block = local_points // lax.axis_size("member")
    upper = jnp.asarray(np.triu(np.ones((members, members), np.float32), 1))
    spread_rows = lax.all_to_all(predicted, "member", split_axis=2, concat_axis=0, tiled=True)
    gap = spread_rows[:, None] - spread_rows[None]
    soft_abs = jnp.sqrt(gap * gap + soft_square)
    sign_total = jnp.sum(gap / soft_abs, axis=1)
    abs_total = jnp.sum(soft_abs * upper[:, :, None, None], axis=(0, 1))
    returned = lax.all_to_all(sign_total, "member", split_axis=0, concat_axis=2, tiled=True)
    pair_abs = abs_total[None]
    lat_block = lax.dynamic_slice_in_dim(lat_weight, lax.axis_index("member") * block, block)
    pair_loss = jnp.sum(pair_abs[0] * var_weight[:, None] * lat_block[None, :])
    obs_loss = jnp.sum(jnp.sum(obs_abs, axis=0) * weight_grid)
    loss_part = obs_loss / members - pair_loss * scale_pair
    grad_pred = (weight_grid[None] * (obs_sign / members - returned * scale_pair)).astype(
        jnp.bfloat16
    )
    points_total = local_points * lax.axis_size("grid")
    factor = points_total / lat_total
    grad_normed = jnp.einsum("rvp,vd->rpd", grad_pred, weight, preferred_element_type=jnp.float32)
    grad_unit = grad_normed * gain[None, None, :]
    mean_one = jnp.mean(grad_unit, axis=-1, keepdims=True)
    mean_two = jnp.mean(grad_unit * unit_rows, axis=-1, keepdims=True)
    grad_fields = (factor * (inv_std * (grad_unit - mean_one - unit_rows * mean_two))).astype(
        jnp.bfloat16
    )
    part_weight = jnp.einsum("rvp,rpd->vd", grad_pred, normed, preferred_element_type=jnp.float32)
    part_gain = jnp.sum(grad_normed * unit_rows, axis=(0, 1))
    part_bias = jnp.sum(grad_pred.astype(jnp.float32), axis=(0, 2))
    grad_weight, grad_gain, grad_bias, loss_total = lax.psum(
        (part_weight, part_gain, part_bias, loss_part), ("grid", "member")
    )
    variables = observed.shape[0]
    loss = loss_total / (variables * lat_total)
    return (grad_fields, factor * grad_weight, factor * grad_gain, factor * grad_bias, loss)


def solution(mesh):
    return jax.shard_map(
        shards,
        mesh=mesh,
        in_specs=(P("member", "grid", None), P(None, "grid"), P("grid"), P(), P(), P(), P()),
        out_specs=(P("member", "grid", None), P(), P(), P(), P()),
        check_vma=False,
    )
```

profile of v0, /device:TPU:1, one launch (start us, length us, event | category | flops | bytes accessed | tf_op | source)
XLA Modules:
  0.0 498.5 jit_solution(1338902217500725341)
XLA Ops:
  7.2 0.0 copy-start
  7.2 0.0 copy-start.5
  7.2 0.0 copy-start.4
  7.2 0.0 copy-start.6
  7.2 0.0 copy-start.3
  7.2 0.0 copy-start.7
  7.2 3.0 copy.30
  10.2 0.4 convert_reduce_fusion
  10.6 0.6 fusion.13
  11.2 0.0 copy-done
  11.2 0.0 copy-done.5
  11.3 0.0 copy-done.4
  11.3 0.0 copy-done.6
  11.3 0.0 copy-done.3
  11.3 0.0 copy-done.7
  11.3 0.0 copy-start.8
  11.3 1.6 fusion.22
  12.9 0.0 copy-start.1
  12.9 0.8 copy-done.1
  13.6 0.3 copy.31
  14.0 25.4 %all_to_all.24 = f32[1,100,1024]{1,0,2:T(1,128)S(1)} all-to-all(f32[1,100,1024]{1,0,2:T(1,128)S(1)} %copy.31), channel_id=1, replica_groups=mesh['grid'=64,'member'=8] {'member'}, dimensions={2} | all-to-all | bytes 819200 | tf_op jit(solution)/shard_map/all_to_all | solution.py:39
  39.4 0.0 copy-start.2
  39.4 2.2 copy.32
  41.6 1.1 copy.33
  42.7 0.0 copy-done.8
  42.7 4.7 fusion.18
  47.4 4.1 all-to-all-start.1
  51.5 0.0 all-reduce.3.cloned.1.call-start
  51.5 0.6 reduce_sum.105
  52.1 135.5 %psum.35 = f32[]{:T(128)} all-reduce(f32[]{:T(128)} %reduce_sum.105), channel_id=1, replica_groups=mesh['grid'=64,'member'=8] {'grid'}, use_global_device_ids=true, to_apply=%region_1.0 | all-reduce | flops 1 | bytes 8 | tf_op jit(solution)/shard_map/psum | solution.py:30
  188.9 0.1 dynamic_slice.3
  189.7 0.7 multiply_reduce_fusion.1
  191.0 0.0 all-to-all-done.1
  191.1 0.1 copy.34
  191.2 0.0 copy-done.2
  191.2 1.3 convert_reduce_fusion.1
  192.5 1.7 fusion.25
  194.2 3.3 fusion.12
  197.5 0.0 all-reduce.3.cloned.1.call-update
  197.5 2.5 multiply_reduce_fusion
  200.1 123.6 %all-reduce = (f32[1024]{0:T(1024)S(1)}, f32[100]{0:T(128)S(1)}, f32[]{:T(128)}) all-reduce(f32[1024]{0:T(1024)S(1)} %get-tuple-element.25, f32[100]{0:T(128)S(1)} %get-tuple-element.32, f32[]{:T(128)S(6)} %sub.58), channel_id=1, replica_groups=mesh['grid'=64,'member'=8] {'grid','member'}, use_global_device_ids=true, to_apply=%region_9.0 | all-reduce | flops 1125 | bytes 9000 | tf_op jit(solution)/shard_map/psum | solution.py:65
  323.6 0.6 broadcast_multiply_fusion.1
  324.2 4.8 fusion.11
  329.1 3.9 copy.36
  333.7 0.5 broadcast_multiply_fusion.5
  334.2 154.6 %all-reduce.3.cloned.1.call-done = f32[100,1024]{1,0:T(8,128)} async-done(((f32[100,1024]{1,0:T(8,128)}), f32[100,1024]{1,0:T(8,128)}) %all-reduce.3.cloned.1.call-update) | async-done | bytes 409616 | tf_op jit(solution)/shard_map/psum | solution.py:65
  488.7 1.8 broadcast_multiply_fusion
  (5 shorter events, 0.1 us)
Async XLA Ops:
  7.2 4.1 copy-start
  7.2 4.1 copy-start.5
  7.2 4.1 copy-start.4
  7.2 4.1 copy-start.6
  7.2 4.1 copy-start.3
  7.2 4.1 copy-start.7
  11.3 31.4 %copy-start.8 = (f32[8,8]{1,0:T(8,128)S(1)}, f32[8,8]{1,0:T(8,128)}, u32[]{:S(2)}) copy-start(f32[8,8]{1,0:T(8,128)} %constant.37.clone) | copy-start | bytes 772
  12.9 0.8 copy-start.1
  39.4 151.7 %copy-start.2 = (f32[1,100,1024]{2,1,0:T(8,128)S(1)}, f32[1,100,1024]{2,1,0:T(8,128)}, u32[]{:S(2)}) copy-start(f32[1,100,1024]{2,1,0:T(8,128)} %copy-done.1) | copy-start | bytes 1228804
  47.4 143.6 %all-to-all-start.1 = ((f32[8,100,128]{2,1,0:T(8,128)}), f32[8,100,128]{2,1,0:T(8,128)S(1)}, u32[]{:S(2)}, u32[]{:S(2)}) async-start(f32[8,100,128]{2,1,0:T(8,128)} %get-tuple-element.28), calls=%async_computation.1 | async-start | bytes 851968 | tf_op jit(solution)/shard_map/all_to_all | solution.py:44
  51.5 437.2 %all-reduce.3.cloned.1.call-start = ((), (), s32[]{:S(2)}) async-start(), calls=%async_computation.2 | async-start | bytes 851968 | tf_op jit(solution)/shard_map/psum | solution.py:65
Sparse Core Ops, SparseCore 0:
  197.6 291.0 all-reduce.2
where the time goes:
time: 499 us
  blocking collectives  285 us (57%)
  waiting for transfers between devices  155 us (31%)
  other arithmetic  18.7 us (4%)
  between operations  18.7 us (4%)
  local copies, waits for them, and re-layouts  11.5 us (2%)
  matrix products  6.53 us (1%)
    psum x1, waiting for transfers between devices, shards(): lax.psum((part_weight, part_gain, part_bias, loss_part), ('grid', 'member'))  155 us
    psum x1, blocking collectives, shards(): lat_total = lax.psum(jnp.sum(lat_weight), 'grid')  136 us
    psum x1, blocking collectives, shards(): lax.psum((part_weight, part_gain, part_bias, loss_part), ('grid', 'member'))  124 us
    all_to_all x1, blocking collectives, shards(): lax.all_to_all(predicted, 'member', split_axis=2, concat_axis=0, tiled=True)  25.4 us
  transfers between devices with their start and end apart: 2, of which 1 were waited for; matrix products, arithmetic and copies ran while one was open for 3% of the time, Pallas kernels for 0%

commit v1 on v0

v1 whole, which is shorter than its diff:
```python
import functools
import jax
import jax.numpy as jnp
from jax import lax
from jax.experimental import pallas as pl
from jax.experimental.pallas import tpu as pltpu
from jax.sharding import Mesh, PartitionSpec as P

soft_square = 0.01
norm_epsilon = 1e-05

V = 100
M = 8
D = 1024
LOCAL = 1024
LANES = 128
ROWS = 104
GAIN_ROW, MISC_ROW, LAT_ROW = 100, 101, 102
XC = ("x", "core")
YZ = ("y_lo", "y_hi", "z")
MEMBER = ("y_hi", "core")
VMEM_LIMIT = 20 * 1024 * 1024
f32, bf16 = jnp.float32, jnp.bfloat16
NT = (((1,), (1,)), ((), ()))
TN = (((0,), (0,)), ((), ()))


def params(**kw):
    return pltpu.CompilerParams(vmem_limit_bytes=VMEM_LIMIT, **kw)


def column(row):
    n = row.shape[1]
    if n < LANES:
        row = jnp.concatenate([row, jnp.zeros((1, LANES - n), row.dtype)], axis=1)
    return jnp.broadcast_to(row, (LANES, LANES)).T


def unit_of(values):
    row_mean = jnp.mean(values, axis=-1, keepdims=True)
    centred = values - row_mean
    inv_std = lax.rsqrt(jnp.mean(centred * centred, axis=-1, keepdims=True) + norm_epsilon)
    return centred * inv_std, inv_std


def forward_kernel(fields_ref, weight_ref, bias_ref, gain_ref, pred_ref, normed_ref, resid_ref):
    unit, _ = unit_of(fields_ref[...].astype(f32))
    scaled = unit * gain_ref[...]
    normed = scaled.astype(bf16)
    normed_ref[...] = normed
    resid_ref[...] = (scaled - normed.astype(f32)).astype(bf16)
    pred = lax.dot_general(weight_ref[...], normed, NT, preferred_element_type=f32)
    bias = column(bias_ref[...])[:V]
    for k in range(pred_ref.shape[0]):
        pred_ref[k] = pred[:, k * LANES : (k + 1) * LANES] + bias


def forward(fields, weight, bias, gain, tile=256):
    slots = tile // LANES
    return pl.pallas_call(
        forward_kernel,
        grid=(LOCAL // tile,),
        in_specs=[
            pl.BlockSpec((tile, D), lambda i: (i, 0)),
            pl.BlockSpec((V, D), lambda i: (0, 0)),
            pl.BlockSpec((1, V), lambda i: (0, 0)),
            pl.BlockSpec((1, D), lambda i: (0, 0)),
        ],
        out_specs=[
            pl.BlockSpec((slots, V, LANES), lambda i: (i, 0, 0)),
            pl.BlockSpec((tile, D), lambda i: (i, 0)),
            pl.BlockSpec((tile, D), lambda i: (i, 0)),
        ],
        out_shape=[
            jax.ShapeDtypeStruct((M, V, LANES), f32),
            jax.ShapeDtypeStruct((LOCAL, D), bf16),
            jax.ShapeDtypeStruct((LOCAL, D), bf16),
        ],
        compiler_params=params(),
        cost_estimate=pl.CostEstimate(flops=2 * V * D * LOCAL, bytes_accessed=8 << 20, transcendentals=0),
    )(fields, weight, bias, gain)


def pair_kernel(slot_ref, pred_ref, obs_ref, lat_ref, vw_ref, grad_ref, loss_ref):
    del slot_ref
    vw = column(vw_ref[...])
    lat = lat_ref[...].reshape(1, LANES)
    loss = jnp.zeros((8, LANES), f32)
    for start in range(0, V, 8):
        rows = min(8, V - start)
        part = slice(start, start + rows)
        obs = obs_ref[part].astype(f32)
        pred = [pred_ref[m, part] for m in range(M)]
        sign = [None] * M
        pair_abs = None
        obs_abs = None
        for m in range(M):
            gap = pred[m] - obs
            square = gap * gap + soft_square
            inverse = lax.rsqrt(square)
            size = square * inverse
            obs_abs = size if obs_abs is None else obs_abs + size
            sign[m] = gap * inverse * float(M - 1)
        for i in range(M):
            for j in range(i + 1, M):
                gap = pred[i] - pred[j]
                square = gap * gap + soft_square
                inverse = lax.rsqrt(square)
                size = square * inverse
                pair_abs = size if pair_abs is None else pair_abs + size
                term = gap * inverse
                sign[i] = sign[i] - term
                sign[j] = sign[j] + term
        scale = vw[part] * lat
        crps = obs_abs * (1.0 / M) - pair_abs * (1.0 / (M * (M - 1)))
        crps = crps * scale
        if rows < 8:
            crps = jnp.concatenate([crps, jnp.zeros((8 - rows, LANES), f32)], axis=0)
        loss = loss + crps
        scale = scale * (1.0 / (M * (M - 1)))
        for m in range(M):
            grad_ref[m, part] = sign[m] * scale
    loss_ref[...] = loss


def pair(slot, pred, observed, lat, var_weight):
    return pl.pallas_call(
        pair_kernel,
        grid_spec=pltpu.PrefetchScalarGridSpec(
            num_scalar_prefetch=1,
            grid=(1,),
            in_specs=[
                pl.BlockSpec((M, V, LANES), lambda i, s: (0, 0, 0)),
                pl.BlockSpec((V, LANES), lambda i, s: (0, s[0])),
                pl.BlockSpec((1, 1, LANES), lambda i, s: (s[0], 0, 0)),
                pl.BlockSpec((1, V), lambda i, s: (0, 0)),
            ],
            out_specs=[
                pl.BlockSpec((M, V, LANES), lambda i, s: (0, 0, 0)),
                pl.BlockSpec((8, LANES), lambda i, s: (0, 0)),
            ],
        ),
        out_shape=[
            jax.ShapeDtypeStruct((M, V, LANES), f32),
            jax.ShapeDtypeStruct((8, LANES), f32),
        ],
        compiler_params=params(),
    )(slot, pred, observed, lat, var_weight)


def weight_kernel(grad_ref, normed_ref, resid_ref, weight_ref, gain_ref, lat_ref, loss_ref, out_ref, total_ref, rest_ref, sums_ref):
    step = pl.program_id(0)
    slots = grad_ref.shape[0]
    grad = jnp.concatenate([grad_ref[k] for k in range(slots)], axis=1).astype(bf16)
    total = jnp.dot(grad, normed_ref[...], preferred_element_type=f32)
    rest = jnp.dot(grad, resid_ref[...], preferred_element_type=f32)
    ones = jnp.ones((8, grad.shape[1]), bf16)
    sums = lax.dot_general(ones, grad, NT, preferred_element_type=f32)

    @pl.when(step == 0)
    def _():
        total_ref[...] = total
        rest_ref[...] = rest
        sums_ref[...] = sums

    @pl.when(step > 0)
    def _():
        total_ref[...] += total
        rest_ref[...] += rest
        sums_ref[...] += sums

    @pl.when(step == pl.num_programs(0) - 1)
    def _():
        total = total_ref[...]
        part = weight_ref[...].astype(f32) * (total + rest_ref[...])
        part_gain = jnp.sum(part, axis=0, keepdims=True) / gain_ref[...]
        lane = lax.broadcasted_iota(jnp.int32, (1, LANES), 1)
        bias_row = jnp.concatenate([sums_ref[0:1], jnp.zeros((1, LANES - V), f32)], axis=1)
        loss = jnp.sum(loss_ref[...], keepdims=True)
        misc = jnp.where(lane == V, loss, bias_row)
        lat = jnp.broadcast_to(jnp.sum(lat_ref[...], keepdims=True), (1, LANES))
        tail = jnp.concatenate([misc, lat, jnp.zeros((1, LANES), f32)], axis=0)
        for k in range(M):
            cols = slice(k * LANES, (k + 1) * LANES)
            out_ref[k, :V] = total[:, cols]
            out_ref[k, V:] = jnp.concatenate([part_gain[:, cols], tail], axis=0)


def weight_part(grad, normed, resid, weight, gain, lat, loss, tile=256):
    slots = tile // LANES
    return pl.pallas_call(
        weight_kernel,
        grid=(LOCAL // tile,),
        in_specs=[
            pl.BlockSpec((slots, V, LANES), lambda i: (i, 0, 0)),
            pl.BlockSpec((tile, D), lambda i: (i, 0)),
            pl.BlockSpec((tile, D), lambda i: (i, 0)),
            pl.BlockSpec((V, D), lambda i: (0, 0)),
            pl.BlockSpec((1, D), lambda i: (0, 0)),
            pl.BlockSpec((M, LANES), lambda i: (0, 0)),
            pl.BlockSpec((8, LANES), lambda i: (0, 0)),
        ],
        out_specs=pl.BlockSpec((M, ROWS, LANES), lambda i: (0, 0, 0)),
        out_shape=jax.ShapeDtypeStruct((M, ROWS, LANES), f32),
        scratch_shapes=[pltpu.VMEM((V, D), f32), pltpu.VMEM((V, D), f32), pltpu.VMEM((8, V), f32)],
        compiler_params=params(),
    )(grad, normed, resid, weight, gain, lat, loss)


def fold_kernel(parts_ref, out_ref):
    total = parts_ref[0]
    for k in range(1, M):
        total = total + parts_ref[k]
    total = jnp.concatenate([total, jnp.zeros((LANES - ROWS, LANES), f32)], axis=0)
    out_ref[...] = total.T


def fold(parts):
    return pl.pallas_call(
        fold_kernel,
        out_shape=jax.ShapeDtypeStruct((LANES, LANES), f32),
        compiler_params=params(),
    )(parts)


def share_kernel(parts_ref, out_ref, lat_ref):
    total = jnp.sum(parts_ref[...], axis=0)
    out_ref[...] = jnp.broadcast_to(total[None], out_ref.shape)
    lat_ref[...] = jnp.broadcast_to(total[0:1, LAT_ROW : LAT_ROW + 1] * (1.0 / M), (8, LANES))


def share(parts):
    return pl.pallas_call(
        share_kernel,
        out_shape=[
            jax.ShapeDtypeStruct(parts.shape, f32),
            jax.ShapeDtypeStruct((8, LANES), f32),
        ],
        compiler_params=params(),
    )(parts)


def spread_kernel(parts_ref, out_ref):
    total = parts_ref[...].T[:ROWS]
    out_ref[...] = jnp.broadcast_to(total[None], out_ref.shape)


def spread(parts):
    return pl.pallas_call(
        spread_kernel,
        out_shape=jax.ShapeDtypeStruct((M, ROWS, LANES), f32),
        compiler_params=params(),
    )(parts)


def finish_kernel(points_total, parts_ref, weight_ref, gain_ref, bias_ref, loss_ref):
    lat_total = parts_ref[0, LAT_ROW : LAT_ROW + 1, 0:1] * (1.0 / M)
    factor = points_total / lat_total
    for k in range(M):
        cols = slice(k * LANES, (k + 1) * LANES)
        weight_ref[:, cols] = parts_ref[k, :V] * factor
        gain_ref[:, cols] = parts_ref[k, GAIN_ROW : GAIN_ROW + 1] * factor
    misc = parts_ref[0, MISC_ROW : MISC_ROW + 1]
    bias_ref[...] = misc[:, :V] * factor
    loss_ref[...] = misc[:, V : V + 1] / (V * lat_total)


def finish(parts, points_total):
    return pl.pallas_call(
        functools.partial(finish_kernel, points_total),
        out_shape=[
            jax.ShapeDtypeStruct((V, D), f32),
            jax.ShapeDtypeStruct((1, D), f32),
            jax.ShapeDtypeStruct((1, V), f32),
            jax.ShapeDtypeStruct((1, 1), f32),
        ],
        compiler_params=params(),
    )(parts)


def fields_kernel(points_total, fields_ref, grad_ref, weight_ref, gain_ref, lat_ref, out_ref):
    unit, inv_std = unit_of(fields_ref[...].astype(f32))
    slots = grad_ref.shape[0]
    grad = jnp.concatenate([grad_ref[k] for k in range(slots)], axis=1).astype(bf16)
    grad_normed = lax.dot_general(grad, weight_ref[...], TN, preferred_element_type=f32)
    grad_unit = grad_normed * gain_ref[...]
    mean_one = jnp.mean(grad_unit, axis=-1, keepdims=True)
    mean_two = jnp.mean(grad_unit * unit, axis=-1, keepdims=True)
    factor = points_total / lat_ref[0:1, 0:1]
    out_ref[...] = ((factor * inv_std) * (grad_unit - mean_one - unit * mean_two)).astype(bf16)


def fields_part(fields, grad, weight, gain, lat_total, points_total, tile=256):
    slots = tile // LANES
    return pl.pallas_call(
        functools.partial(fields_kernel, points_total),
        grid=(LOCAL // tile,),
        in_specs=[
            pl.BlockSpec((tile, D), lambda i: (i, 0)),
            pl.BlockSpec((slots, V, LANES), lambda i: (i, 0, 0)),
            pl.BlockSpec((V, D), lambda i: (0, 0)),
            pl.BlockSpec((1, D), lambda i: (0, 0)),
            pl.BlockSpec((8, LANES), lambda i: (0, 0)),
        ],
        out_specs=pl.BlockSpec((tile, D), lambda i: (i, 0)),
        out_shape=jax.ShapeDtypeStruct((LOCAL, D), bf16),
        compiler_params=params(),
        cost_estimate=pl.CostEstimate(flops=2 * V * D * LOCAL, bytes_accessed=5 << 20, transcendentals=0),
    )(fields, grad, weight, gain, lat_total)


def swap(array, axes):
    return lax.all_to_all(array, axes, split_axis=0, concat_axis=0, tiled=True)


def shards(points_total, fields, observed, lat_weight, var_weight, weight, bias, gain):
    fields = fields.reshape(LOCAL, D)
    gain_row = gain.reshape(1, D)
    slot = lax.axis_index(MEMBER).astype(jnp.int32).reshape(1)
    pred, normed, resid = forward(fields, weight, bias.reshape(1, V), gain_row)
    pred = swap(pred, MEMBER)
    grad, loss = pair(slot, pred, observed, lat_weight.reshape(M, 1, LANES), var_weight.reshape(1, V))
    grad = swap(grad, MEMBER)
    parts = weight_part(grad, normed, resid, weight, gain_row, lat_weight.reshape(M, LANES), loss)
    parts = swap(parts, XC)
    parts = fold(parts).reshape(64, 2, LANES)
    parts = swap(parts, YZ)
    parts, lat_total = share(parts)
    parts = swap(parts, YZ)
    grad_fields = fields_part(fields, grad, weight, gain_row, lat_total, points_total)
    parts = spread(parts.reshape(LANES, LANES))
    parts = swap(parts, XC)
    grad_weight, grad_gain, grad_bias, loss = finish(parts, points_total)
    return (
        grad_fields.reshape(1, LOCAL, D),
        grad_weight,
        grad_gain.reshape(D),
        grad_bias.reshape(V),
        loss.reshape(()),
    )


def solution(mesh):
    devices = mesh.devices.reshape(4, 2, 8, 4, 2)
    fine = Mesh(devices, ("x", "y_lo", "z", "y_hi", "core"))
    grid = ("x", "y_lo", "z")
    points_total = float(LOCAL * 64)
    return jax.shard_map(
        functools.partial(shards, points_total),
        mesh=fine,
        in_specs=(P(MEMBER, grid, None), P(None, grid), P(grid), P(), P(), P(), P()),
        out_specs=(P(MEMBER, grid, None), P(), P(), P(), P()),
        check_vma=False,
    )
```

time: 499 us -> 123 us (0.25)
  blocking collectives: 285 us -> 69 us
  waiting for transfers between devices: 155 us -> 18 us
  other arithmetic: 18.7 us -> 0 us
  between operations: 18.7 us -> 0.72 us
  starting transfers between devices: 4.11 us -> 17.1 us
  Pallas kernels: 0 us -> 10.4 us
  matrix products: 6.53 us -> 0 us
    psum x2 -> x0, blocking collectives: 259 us -> none  [the longest x1 136 us: shards(): lat_total = lax.psum(jnp.sum(lat_weight), 'grid')]
    psum x1 -> x0, waiting for transfers between devices: 155 us -> none  [shards(): lax.psum((part_weight, part_gain, part_bias, loss_part), ('grid', 'member'))]
    all_to_all x1 -> x4, blocking collectives: 25.4 us -> 69 us  [swap(): return lax.all_to_all(array, axes, split_axis=0, concat_axis=0, tiled=True)]
    all_to_all x1 -> x2, waiting for transfers between devices: 0.01 us -> 18 us  [swap(): return lax.all_to_all(array, axes, split_axis=0, concat_axis=0, tiled=True)]
    all_to_all x1 -> x2, starting transfers between devices: 4.11 us -> 17.1 us  [swap(): return lax.all_to_all(array, axes, split_axis=0, concat_axis=0, tiled=True)]
    reduce_sum x7 -> x0, other arithmetic: 10.8 us -> none  [the longest x1 4.71 us: shards(): abs_total = jnp.sum(soft_abs * upper[:, :, None, None], axis=(0, 1))]
    pallas_call x0 -> x8, Pallas kernels: none -> 10.4 us  [the longest x1 3.74 us: fields_part(): pl.pallas_call(functools.partial(fields_kernel, points_total), grid=(LOCA...]
    dot_general x3 -> x0, matrix products: 6.53 us -> none  [the longest x1 3.29 us: shards(): jnp.einsum('rvp,vd->rpd', grad_pred, weight, preferred_element_type=jnp.f...]
  transfers between devices with their start and end apart: 2 -> 2, of which waited for: 1 -> 2; matrix products, arithmetic and copies ran while one was open for 3% -> 0% of each run, Pallas kernels for 0% -> 3%
where the time goes in v1:
time: 123 us
  blocking collectives  69 us (56%)
  waiting for transfers between devices  18 us (15%)
  starting transfers between devices  17.1 us (14%)
  Pallas kernels  10.4 us (8%)
  local copies, waits for them, and re-layouts  7.56 us (6%)
    all_to_all x4, blocking collectives, swap(): return lax.all_to_all(array, axes, split_axis=0, concat_axis=0, tiled=True)  69 us
    all_to_all x2, waiting for transfers between devices, swap(): return lax.all_to_all(array, axes, split_axis=0, concat_axis=0, tiled=True)  18 us
    all_to_all x2, starting transfers between devices, swap(): return lax.all_to_all(array, axes, split_axis=0, concat_axis=0, tiled=True)  17.1 us
    unnamed x26, local copies, waits for them, and re-layouts  7.56 us
    pallas_call x1, Pallas kernels, fields_part(): pl.pallas_call(functools.partial(fields_kernel, points_total), grid=(LOCA...  3.74 us
    pallas_call x1, Pallas kernels, forward(): pl.pallas_call(forward_kernel, grid=(LOCAL // tile,), in_specs=[pl.BlockS...  3.12 us
  transfers between devices with their start and end apart: 2, of which 2 were waited for; matrix products, arithmetic and copies ran while one was open for 0% of the time, Pallas kernels for 3%

profile of v1, /device:TPU:1, one launch (start us, length us, event | category | flops | bytes accessed | tf_op | source)
XLA Modules:
  0.0 122.8 jit_solution(13356113774892516976)
XLA Ops:
  0.6 0.0 copy-start.10
  0.6 0.0 copy-start.12
  0.7 0.0 copy-start
  0.7 1.6 %copy-done = bf16[1,1024,1024]{2,1,0:T(8,128)(2,1)S(1)} copy-done((bf16[1,1024,1024]{2,1,0:T(8,128)(2,1)S(1)}, bf16[1,1024,1024]{2,1,0:T(8,128)(2,1)}, u32[]{:S(2)}) %copy-start) | copy-done | bytes 2097176
  2.3 0.0 copy-start.4
  2.3 0.9 copy-done.4
  3.2 0.0 copy-start.8
  3.2 0.7 copy-done.8
  3.9 0.0 copy-start.11
  3.9 0.7 copy-done.11
  4.5 0.0 copy-start.7
  4.5 0.0 copy-start.5
  4.5 0.0 copy-start.9
  4.5 3.1 %shard_map.110 = (f32[8,100,128]{2,1,0:T(8,128)}, bf16[1024,1024]{1,0:T(8,128)(2,1)S(1)}, bf16[1024,1024]{1,0:T(8,128)(2,1)S(1)}) custom-call(bf16[1024,1024]{1,0:T(8,128)(2,1)S(1)} %bitcast.13, bf16[100,1024]{1,0:T(8,128)(2,1)S(1)} %copy-done.4, f32[1,100]{1,0:T(1,128)S(1)} %bitcast.22, f32[1,1024]{1,0:T(1,128)S(1)} %bitcast.17), custom_call_target="tpu_custom_call" | custom-call | flops 209715200 | bytes 8388608 | tf_op jit(solution)/shard_map/pallas_call | solution.py:60
  7.7 0.0 copy-start.2
  7.7 1.3 %copy-done.2 = bf16[1024,1024]{1,0:T(8,128)(2,1)} copy-done((bf16[1024,1024]{1,0:T(8,128)(2,1)}, bf16[1024,1024]{1,0:T(8,128)(2,1)S(1)}, u32[]{:S(2)}) %copy-start.2) | copy-done | bytes 2097176
  9.0 10.2 %all-to-all-start = ((f32[8,100,128]{2,1,0:T(8,128)}), f32[8,100,128]{2,1,0:T(8,128)S(1)}, u32[]{:S(2)}, u32[]{:S(2)}) async-start(f32[8,100,128]{2,1,0:T(8,128)} %get-tuple-element.16), calls=%async_computation | async-start | bytes 851968 | tf_op jit(solution)/shard_map/all_to_all | solution.py:313
  19.2 13.3 %all-to-all-done.pred_ref = f32[8,100,128]{2,1,0:T(8,128)S(1)} async-done(((f32[8,100,128]{2,1,0:T(8,128)}), f32[8,100,128]{2,1,0:T(8,128)S(1)}, u32[]{:S(2)}, u32[]{:S(2)}) %all-to-all-start) | async-done | bytes 409632 | tf_op jit(solution)/shard_map/all_to_all | solution.py:313
  32.5 0.0 copy-done.10
  32.5 0.0 copy-done.12
  32.5 0.0 copy-done.7
  32.5 0.6 shard_map.111
  33.1 16.2 %all_to_all.30.grad_ref = f32[8,100,128]{2,1,0:T(8,128)S(1)} all-to-all(f32[8,100,128]{2,1,0:T(8,128)S(1)} %get-tuple-element.17), channel_id=1, replica_groups=mesh['x'=4,'y_lo'=2,'z'=8,'y_hi'=4,'core'=2] {'y_hi','core'}, dimensions={0} | all-to-all | bytes 819200 | tf_op jit(solution)/shard_map/all_to_all | solution.py:313
  49.3 0.0 copy-done.5
  49.3 0.0 copy-done.9
  49.3 0.0 copy-start.3
  49.3 1.6 %copy-done.3 = bf16[1024,1024]{1,0:T(8,128)(2,1)S(1)} copy-done((bf16[1024,1024]{1,0:T(8,128)(2,1)S(1)}, bf16[1024,1024]{1,0:T(8,128)(2,1)}, u32[]{:S(2)}) %copy-start.3) | copy-done | bytes 2097176
  50.9 1.8 %shard_map.112 = f32[8,104,128]{2,1,0:T(8,128)S(1)} custom-call(f32[8,100,128]{2,1,0:T(8,128)S(1)} %all_to_all.30.grad_ref, bf16[1024,1024]{1,0:T(8,128)(2,1)S(1)} %get-tuple-element.18.normed_ref, bf16[1024,1024]{1,0:T(8,128)(2,1)S(1)} %copy-done.3, bf16[100,1024]{1,0:T(8,128)(2,1)S(1)} %copy-done.5, f32[1,1024]{1,0:T(1,128)S(1)} %bitcast.18, ...), custom_call_target="tpu_custom_call" | custom-call | tf_op jit(solution)/shard_map/pallas_call | solution.py:191
  52.7 0.0 copy-start.1
  52.7 15.7 %all_to_all.31.parts_ref = f32[8,104,128]{2,1,0:T(8,128)S(1)} all-to-all(f32[8,104,128]{2,1,0:T(8,128)S(1)} %shard_map.112), channel_id=1, replica_groups=mesh['x'=4,'y_lo'=2,'z'=8,'y_hi'=4,'core'=2] {'x','core'}, dimensions={0} | all-to-all | bytes 851968 | tf_op jit(solution)/shard_map/all_to_all | solution.py:313
  68.4 0.1 shard_map.113
  68.5 22.2 %all_to_all.32.parts_ref = f32[64,2,128]{2,1,0:T(2,128)S(1)} all-to-all(f32[64,2,128]{2,1,0:T(2,128)S(1)} %bitcast.15), channel_id=1, replica_groups=mesh['x'=4,'y_lo'=2,'z'=8,'y_hi'=4,'core'=2] {'y_lo','y_hi','z'}, dimensions={0} | all-to-all | bytes 131072 | tf_op jit(solution)/shard_map/all_to_all | solution.py:313
  90.7 0.2 shard_map.114
  90.8 15.0 %all_to_all.33 = f32[64,2,128]{2,1,0:T(2,128)S(1)} all-to-all(f32[64,2,128]{2,1,0:T(2,128)S(1)} %get-tuple-element.22), channel_id=1, replica_groups=mesh['x'=4,'y_lo'=2,'z'=8,'y_hi'=4,'core'=2] {'y_lo','y_hi','z'}, dimensions={0} | all-to-all | bytes 131072 | tf_op jit(solution)/shard_map/all_to_all | solution.py:313
  105.8 0.1 shard_map.116
  105.9 0.0 copy-start.6
  105.9 0.7 copy-done.6
  106.7 6.8 %all-to-all-start.5 = ((f32[8,104,128]{2,1,0:T(8,128)}), f32[8,104,128]{2,1,0:T(8,128)S(1)}, u32[]{:S(2)}, u32[]{:S(2)}) async-start(f32[8,104,128]{2,1,0:T(8,128)} %copy-done.6), calls=%async_computation.5 | async-start | bytes 851968 | tf_op jit(solution)/shard_map/all_to_all | solution.py:313
  113.5 0.0 copy-done.1
  113.5 3.7 %shard_map.115 = bf16[1024,1024]{1,0:T(8,128)(2,1)} custom-call(bf16[1024,1024]{1,0:T(8,128)(2,1)S(1)} %bitcast.14, f32[8,100,128]{2,1,0:T(8,128)S(1)} %all_to_all.30.grad_ref, bf16[100,1024]{1,0:T(8,128)(2,1)S(1)} %copy-done.5, f32[1,1024]{1,0:T(1,128)S(1)} %bitcast.19, f32[8,128]{1,0:T(8,128)S(1)} %get-tuple-element.21.lat_ref), custom_call_target="tpu_custom_call" | custom-call | flops 209715200 | bytes 5242880 | tf_op jit(solution)/shard_map/pallas_call | solution.py:295
  117.3 4.7 %all-to-all-done.5.parts_ref = f32[8,104,128]{2,1,0:T(8,128)S(1)} async-done(((f32[8,104,128]{2,1,0:T(8,128)}), f32[8,104,128]{2,1,0:T(8,128)S(1)}, u32[]{:S(2)}, u32[]{:S(2)}) %all-to-all-start.5) | async-done | bytes 426016 | tf_op jit(solution)/shard_map/all_to_all | solution.py:313
  122.0 0.9 shard_map.117
Async XLA Ops:
  0.6 31.9 %copy-start.10 = (f32[1024]{0:T(1024)S(1)}, f32[1024]{0:T(1024)}, u32[]{:S(2)}) copy-start(f32[1024]{0:T(1024)} %param.9) | copy-start | bytes 12292
  0.6 31.9 %copy-start.12 = (f32[100]{0:T(128)S(1)}, f32[100]{0:T(128)}, u32[]{:S(2)}) copy-start(f32[100]{0:T(128)} %param.10) | copy-start | bytes 1204
  0.7 1.6 %copy-start = (bf16[1,1024,1024]{2,1,0:T(8,128)(2,1)S(1)}, bf16[1,1024,1024]{2,1,0:T(8,128)(2,1)}, u32[]{:S(2)}) copy-start(bf16[1,1024,1024]{2,1,0:T(8,128)(2,1)} %param.7) | copy-start | bytes 6291460
  2.3 0.9 copy-start.4
  3.2 0.7 copy-start.8
  3.9 0.7 copy-start.11
  4.5 28.0 %copy-start.7 = (bf16[100,1024]{1,0:T(8,128)(2,1)S(1)}, bf16[100,1024]{1,0:T(8,128)(2,1)}, u32[]{:S(2)}) copy-start(bf16[100,1024]{1,0:T(8,128)(2,1)} %obs_ref.1) | copy-start | bytes 614404
  4.5 44.8 %copy-start.5 = (bf16[100,1024]{1,0:T(8,128)(2,1)S(1)}, bf16[100,1024]{1,0:T(8,128)(2,1)}, u32[]{:S(2)}) copy-start(bf16[100,1024]{1,0:T(8,128)(2,1)} %weight_ref.5) | copy-start | bytes 614404
  4.5 44.8 %copy-start.9 = (f32[1024]{0:T(1024)S(1)}, f32[1024]{0:T(1024)}, u32[]{:S(2)}) copy-start(f32[1024]{0:T(1024)} %param.13) | copy-start | bytes 12292
  7.7 1.3 %copy-start.2 = (bf16[1024,1024]{1,0:T(8,128)(2,1)}, bf16[1024,1024]{1,0:T(8,128)(2,1)S(1)}, u32[]{:S(2)}) copy-start(bf16[1024,1024]{1,0:T(8,128)(2,1)S(1)} %get-tuple-element.19.resid_ref) | copy-start | bytes 6291460
  9.0 23.5 %all-to-all-start = ((f32[8,100,128]{2,1,0:T(8,128)}), f32[8,100,128]{2,1,0:T(8,128)S(1)}, u32[]{:S(2)}, u32[]{:S(2)}) async-start(f32[8,100,128]{2,1,0:T(8,128)} %get-tuple-element.16), calls=%async_computation | async-start | bytes 851968 | tf_op jit(solution)/shard_map/all_to_all | solution.py:313
  49.3 1.6 %copy-start.3 = (bf16[1024,1024]{1,0:T(8,128)(2,1)S(1)}, bf16[1024,1024]{1,0:T(8,128)(2,1)}, u32[]{:S(2)}) copy-start(bf16[1024,1024]{1,0:T(8,128)(2,1)} %copy-done.2) | copy-start | bytes 6291460
  52.7 60.8 %copy-start.1 = (bf16[1,1024,1024]{2,1,0:T(8,128)(2,1)S(1)}, bf16[1,1024,1024]{2,1,0:T(8,128)(2,1)}, u32[]{:S(2)}) copy-start(bf16[1,1024,1024]{2,1,0:T(8,128)(2,1)} %param.7) | copy-start | bytes 6291460
  105.9 0.8 copy-start.6
  106.7 15.3 %all-to-all-start.5 = ((f32[8,104,128]{2,1,0:T(8,128)}), f32[8,104,128]{2,1,0:T(8,128)S(1)}, u32[]{:S(2)}, u32[]{:S(2)}) async-start(f32[8,104,128]{2,1,0:T(8,128)} %copy-done.6), calls=%async_computation.5 | async-start | bytes 851968 | tf_op jit(solution)/shard_map/all_to_all | solution.py:313

commit v2 on v1

v2 whole, which is shorter than its diff:
```python
import functools
import jax
import jax.numpy as jnp
from jax import lax
from jax.experimental import pallas as pl
from jax.experimental.pallas import tpu as pltpu
from jax.sharding import Mesh, PartitionSpec as P

soft_square = 0.01
norm_epsilon = 1e-05

V = 100
M = 8
D = 1024
LOCAL = 1024
CHIPS = 256
LANES = 128
TILE = 256
ROWS = 104
GAIN_ROW, MISC_ROW, LAT_ROW = 100, 101, 102
GRID = ("x", "y_lo", "z")
MEMBER = ("y_hi", "core")
CHIP = ("x", "y_lo", "z", "y_hi")
VMEM_LIMIT = 16 * 1024 * 1024
WHOLE_VMEM = 60 * 1024 * 1024
RESIDUAL_VMEM = 62 * 1024 * 1024
VMEM = pl.BlockSpec(memory_space=pltpu.VMEM)
SMEM = pl.BlockSpec(memory_space=pltpu.SMEM)
HBM = pl.BlockSpec(memory_space=pltpu.HBM)
f32, bf16 = jnp.float32, jnp.bfloat16
NT = (((1,), (1,)), ((), ()))
TN = (((0,), (0,)), ((), ()))


def params(limit=VMEM_LIMIT):
    return pltpu.CompilerParams(vmem_limit_bytes=limit)


def column(row):
    n = row.shape[1]
    if n < LANES:
        row = jnp.concatenate([row, jnp.zeros((1, LANES - n), row.dtype)], axis=1)
    return jnp.broadcast_to(row, (LANES, LANES)).T


def unit_of(values):
    row_mean = jnp.mean(values, axis=-1, keepdims=True)
    centred = values - row_mean
    inv_std = lax.rsqrt(jnp.mean(centred * centred, axis=-1, keepdims=True) + norm_epsilon)
    return centred * inv_std, inv_std


def forward_kernel(fields_hbm, weight_hbm, bias_hbm, gain_hbm, pred_hbm, normed_hbm,
                   fields_ref, weight_ref, bias_ref, gain_ref, pred_ref, normed_ref, in_sems, out_sems):
    tiles = LOCAL // TILE
    slots = TILE // LANES
    rows = [pl.ds(t * TILE, TILE) for t in range(tiles)]
    small = [
        pltpu.make_async_copy(gain_hbm, gain_ref, in_sems.at[tiles]),
        pltpu.make_async_copy(weight_hbm, weight_ref, in_sems.at[tiles + 1]),
        pltpu.make_async_copy(bias_hbm, bias_ref, in_sems.at[tiles + 2]),
    ]
    large = [
        pltpu.make_async_copy(fields_hbm.at[rows[t]], fields_ref.at[rows[t]], in_sems.at[t])
        for t in range(tiles)
    ]
    large[0].start()
    for copy in small:
        copy.start()
    for copy in large[1:]:
        copy.start()
    back = []
    for t in range(tiles):
        large[t].wait()
        if t == 0:
            for copy in small:
                copy.wait()
            bias = column(bias_ref[...])[:V]
        unit, _ = unit_of(fields_ref[rows[t]].astype(f32))
        normed = (unit * gain_ref[...]).astype(bf16)
        normed_ref[rows[t]] = normed
        pred = lax.dot_general(weight_ref[...], normed, NT, preferred_element_type=f32)
        for k in range(slots):
            pred_ref[t * slots + k] = pred[:, k * LANES : (k + 1) * LANES] + bias
        here = pl.ds(t * slots, slots)
        back.append(pltpu.make_async_copy(pred_ref.at[here], pred_hbm.at[here], out_sems.at[t, 0]))
        back.append(pltpu.make_async_copy(normed_ref.at[rows[t]], normed_hbm.at[rows[t]], out_sems.at[t, 1]))
        back[-2].start()
        back[-1].start()
    for copy in back:
        copy.wait()


def forward(fields, weight, bias, gain):
    tiles = LOCAL // TILE
    return pl.pallas_call(
        forward_kernel,
        in_specs=[HBM] * 4,
        out_specs=[HBM] * 2,
        out_shape=[
            jax.ShapeDtypeStruct((M, V, LANES), f32),
            jax.ShapeDtypeStruct((LOCAL, D), bf16),
        ],
        scratch_shapes=[
            pltpu.VMEM((LOCAL, D), bf16),
            pltpu.VMEM((V, D), bf16),
            pltpu.VMEM((1, V), f32),
            pltpu.VMEM((1, D), f32),
            pltpu.VMEM((M, V, LANES), f32),
            pltpu.VMEM((LOCAL, D), bf16),
            pltpu.SemaphoreType.DMA((tiles + 3,)),
            pltpu.SemaphoreType.DMA((tiles, 2)),
        ],
        compiler_params=params(WHOLE_VMEM),
        cost_estimate=pl.CostEstimate(flops=2 * V * D * LOCAL, bytes_accessed=6 << 20, transcendentals=0),
    )(fields, weight, bias, gain)


def residual_kernel(fields_ref, gain_ref, normed_ref, out_ref):
    unit, _ = unit_of(fields_ref[...].astype(f32))
    out_ref[...] = (unit * gain_ref[...] - normed_ref[...].astype(f32)).astype(bf16)


def residual(fields, gain, normed):
    block = pl.BlockSpec((TILE, D), lambda i: (i, 0))
    return pl.pallas_call(
        residual_kernel,
        grid=(LOCAL // TILE,),
        in_specs=[block, pl.BlockSpec((1, D), lambda i: (0, 0)), block],
        out_specs=block,
        out_shape=jax.ShapeDtypeStruct((LOCAL, D), bf16),
        compiler_params=params(RESIDUAL_VMEM),
        cost_estimate=pl.CostEstimate(flops=12 * D * LOCAL, bytes_accessed=6 << 20, transcendentals=0),
    )(fields, gain, normed)


def pair_kernel(slot_ref, pred_ref, obs_ref, lat_ref, vw_ref, grad_ref, loss_ref):
    count = pred_ref.shape[1]
    here = pl.ds(pl.multiple_of(slot_ref[0] * LANES, LANES), LANES)
    vw = column(vw_ref[...])
    observed = obs_ref[:, here].astype(f32)
    lat = lat_ref[pl.ds(slot_ref[0], 1), :]
    loss = jnp.zeros((8, LANES), f32)
    for start in range(0, count, 8):
        rows = min(8, count - start)
        part = slice(start, start + rows)
        obs = observed[part]
        pred = [pred_ref[m, part] for m in range(M)]
        sign = [None] * M
        pair_abs = None
        obs_abs = None
        for m in range(M):
            gap = pred[m] - obs
            square = gap * gap + soft_square
            inverse = lax.rsqrt(square)
            size = square * inverse
            obs_abs = size if obs_abs is None else obs_abs + size
            sign[m] = gap * inverse * float(M - 1)
        for i in range(M):
            for j in range(i + 1, M):
                gap = pred[i] - pred[j]
                square = gap * gap + soft_square
                inverse = lax.rsqrt(square)
                size = square * inverse
                pair_abs = size if pair_abs is None else pair_abs + size
                term = gap * inverse
                sign[i] = sign[i] - term
                sign[j] = sign[j] + term
        scale = vw[part] * lat
        crps = obs_abs * (1.0 / M) - pair_abs * (1.0 / (M * (M - 1)))
        crps = crps * scale
        if rows < 8:
            crps = jnp.concatenate([crps, jnp.zeros((8 - rows, LANES), f32)], axis=0)
        loss = loss + crps
        scale = scale * (1.0 / (M * (M - 1)))
        for m in range(M):
            grad_ref[m, part] = sign[m] * scale
    loss_ref[...] = loss


def pair(slot, pred, observed, lat, var_weight):
    return pl.pallas_call(
        pair_kernel,
        in_specs=[SMEM] + [VMEM] * 4,
        out_specs=[pl.BlockSpec(pred.shape, lambda: (0, 0, 0)), VMEM],
        out_shape=[
            jax.ShapeDtypeStruct(pred.shape, f32),
            jax.ShapeDtypeStruct((8, LANES), f32),
        ],
        compiler_params=params(),
        cost_estimate=pl.CostEstimate(flops=1 << 20, bytes_accessed=1 << 19, transcendentals=0),
    )(slot, pred, observed, lat, var_weight)


def weight_kernel(grad_hbm, weight_hbm, gain_hbm, lat_hbm, loss_hbm, normed_hbm, resid_hbm, out_ref,
                  grad_ref, weight_ref, gain_ref, lat_ref, loss_ref, normed_ref, resid_ref, small_sems, sems):
    tiles = LOCAL // TILE
    slots = TILE // LANES
    small = [
        pltpu.make_async_copy(grad_hbm, grad_ref, small_sems.at[0]),
        pltpu.make_async_copy(loss_hbm, loss_ref, small_sems.at[1]),
        pltpu.make_async_copy(lat_hbm, lat_ref, small_sems.at[2]),
        pltpu.make_async_copy(weight_hbm, weight_ref, small_sems.at[3]),
        pltpu.make_async_copy(gain_hbm, gain_ref, small_sems.at[4]),
    ]
    for copy in small:
        copy.start()
    copies = []
    for t in range(tiles):
        rows = pl.ds(t * TILE, TILE)
        copies.append((
            pltpu.make_async_copy(normed_hbm.at[rows], normed_ref.at[rows], sems.at[t, 0]),
            pltpu.make_async_copy(resid_hbm.at[rows], resid_ref.at[rows], sems.at[t, 1]),
        ))
    for copy, _ in copies:
        copy.start()
    for _, copy in copies:
        copy.start()
    for copy in small:
        copy.wait()
    grads = [
        jnp.concatenate([grad_ref[t * slots + k] for k in range(slots)], axis=1).astype(bf16)
        for t in range(tiles)
    ]
    ones = jnp.ones((8, LOCAL), bf16)
    sums = lax.dot_general(ones, jnp.concatenate(grads, axis=1), NT, preferred_element_type=f32)
    loss = jnp.sum(loss_ref[...], keepdims=True)
    lane = lax.broadcasted_iota(jnp.int32, (1, D), 1)
    misc = jnp.concatenate([sums[0:1], jnp.zeros((1, D - V), f32)], axis=1)
    misc = jnp.where(lane == V, loss, misc)
    lat = jnp.broadcast_to(jnp.sum(lat_ref[...], keepdims=True), (1, D))
    total = jnp.zeros((V, D), f32)
    for t in range(tiles):
        copies[t][0].wait()
        rows = pl.ds(t * TILE, TILE)
        total = total + jnp.dot(grads[t], normed_ref[rows], preferred_element_type=f32)
    rest = jnp.zeros((V, D), f32)
    for t in range(tiles):
        copies[t][1].wait()
        rows = pl.ds(t * TILE, TILE)
        rest = rest + jnp.dot(grads[t], resid_ref[rows], preferred_element_type=f32)
    part_gain = jnp.sum(weight_ref[...].astype(f32) * (total + rest), axis=0, keepdims=True) / gain_ref[...]
    out_ref[:V] = total
    out_ref[V:] = jnp.concatenate([part_gain, misc, lat, jnp.zeros((1, D), f32)], axis=0)


def weight_part(grad, weight, gain, lat, loss, normed, resid):
    return pl.pallas_call(
        weight_kernel,
        in_specs=[HBM] * 7,
        out_specs=VMEM,
        out_shape=jax.ShapeDtypeStruct((ROWS, D), f32),
        scratch_shapes=[
            pltpu.VMEM((M, V, LANES), f32),
            pltpu.VMEM((V, D), bf16),
            pltpu.VMEM((1, D), f32),
            pltpu.VMEM((M, LANES), f32),
            pltpu.VMEM((8, LANES), f32),
            pltpu.VMEM((LOCAL, D), bf16),
            pltpu.VMEM((LOCAL, D), bf16),
            pltpu.SemaphoreType.DMA((5,)),
            pltpu.SemaphoreType.DMA((LOCAL // TILE, 2)),
        ],
        compiler_params=params(WHOLE_VMEM),
        cost_estimate=pl.CostEstimate(flops=4 * V * D * LOCAL, bytes_accessed=4 << 20, transcendentals=0),
    )(grad, weight, gain, lat, loss, normed, resid)


def fold_kernel(core_ref, parts_ref, out_ref):
    half = D // 2
    for k in range(half // LANES):
        start = pl.multiple_of(core_ref[0] * half + k * LANES, LANES)
        total = parts_ref[0, :, pl.ds(start, LANES)] + parts_ref[1, :, pl.ds(start, LANES)]
        total = jnp.concatenate([total, jnp.zeros((LANES - ROWS, LANES), f32)], axis=0)
        out_ref[k * LANES : (k + 1) * LANES] = total.T


def fold(core, parts):
    return pl.pallas_call(
        fold_kernel,
        in_specs=[SMEM, VMEM],
        out_specs=VMEM,
        out_shape=jax.ShapeDtypeStruct((D // 2, LANES), f32),
        compiler_params=params(),
    )(core, parts)


def share_kernel(parts_ref, out_ref, lat_ref):
    total = jnp.sum(parts_ref[...].reshape(D // 16, 8, LANES), axis=0)
    total = total + jnp.concatenate([total[4:], total[:4]], axis=0)
    total = total + jnp.concatenate([total[2:], total[:2]], axis=0)
    out_ref[...] = jnp.broadcast_to(total[None], (D // 16, 8, LANES)).reshape(D // 2, LANES)
    lat_ref[...] = jnp.broadcast_to(total[0:1, LAT_ROW : LAT_ROW + 1] * (1.0 / M), (8, LANES))


def share(parts):
    return pl.pallas_call(
        share_kernel,
        in_specs=[VMEM],
        out_specs=[VMEM, VMEM],
        out_shape=[
            jax.ShapeDtypeStruct((D // 2, LANES), f32),
            jax.ShapeDtypeStruct((8, LANES), f32),
        ],
        compiler_params=params(),
    )(parts)


def finish_kernel(points_total, parts_ref, weight_ref, gain_ref, bias_ref, loss_ref):
    lat_total = parts_ref[0:1, LAT_ROW : LAT_ROW + 1] * (1.0 / M)
    factor = points_total / lat_total
    for k in range(D // LANES):
        cols = slice(k * LANES, (k + 1) * LANES)
        block = parts_ref[cols].T
        weight_ref[:, cols] = block[:V] * factor
        gain_ref[:, cols] = block[GAIN_ROW : GAIN_ROW + 1] * factor
        if k == 0:
            misc = block[MISC_ROW : MISC_ROW + 1]
            bias_ref[...] = misc[:, :V] * factor
            loss_ref[...] = misc[:, V : V + 1] / (V * lat_total)


def finish(parts, points_total):
    return pl.pallas_call(
        functools.partial(finish_kernel, points_total),
        in_specs=[VMEM],
        out_shape=[
            jax.ShapeDtypeStruct((V, D), f32),
            jax.ShapeDtypeStruct((1, D), f32),
            jax.ShapeDtypeStruct((1, V), f32),
            jax.ShapeDtypeStruct((1, 1), f32),
        ],
        compiler_params=params(),
    )(parts)


def fields_kernel(points_total, fields_ref, grad_ref, weight_ref, gain_ref, lat_ref, out_ref):
    unit, inv_std = unit_of(fields_ref[...].astype(f32))
    slots = grad_ref.shape[0]
    grad = jnp.concatenate([grad_ref[k] for k in range(slots)], axis=1).astype(bf16)
    grad_normed = lax.dot_general(grad, weight_ref[...], TN, preferred_element_type=f32)
    grad_unit = grad_normed * gain_ref[...]
    mean_one = jnp.mean(grad_unit, axis=-1, keepdims=True)
    mean_two = jnp.mean(grad_unit * unit, axis=-1, keepdims=True)
    factor = points_total / lat_ref[0:1, 0:1]
    out_ref[...] = ((factor * inv_std) * (grad_unit - mean_one - unit * mean_two)).astype(bf16)


def fields_part(fields, grad, weight, gain, lat_total, points_total):
    slots = TILE // LANES
    return pl.pallas_call(
        functools.partial(fields_kernel, points_total),
        grid=(LOCAL // TILE,),
        in_specs=[
            pl.BlockSpec((TILE, D), lambda i: (i, 0)),
            pl.BlockSpec((slots, V, LANES), lambda i: (i, 0, 0)),
            pl.BlockSpec((V, D), lambda i: (0, 0)),
            pl.BlockSpec((1, D), lambda i: (0, 0)),
            pl.BlockSpec((8, LANES), lambda i: (0, 0)),
        ],
        out_specs=pl.BlockSpec((TILE, D), lambda i: (i, 0)),
        out_shape=jax.ShapeDtypeStruct((LOCAL, D), bf16),
        compiler_params=params(),
        cost_estimate=pl.CostEstimate(flops=2 * V * D * LOCAL, bytes_accessed=12 << 20, transcendentals=0),
    )(fields, grad, weight, gain, lat_total)


def swap(array, axes):
    return lax.all_to_all(array, axes, split_axis=0, concat_axis=0, tiled=True)


def shards(points_total, fields, observed, lat_weight, var_weight, weight, bias, gain):
    fields = fields.reshape(LOCAL, D)
    gain_row = gain.reshape(1, D)
    vw_row = var_weight.reshape(1, V)
    lat = lat_weight.reshape(M, LANES)
    slot = lax.axis_index(MEMBER).astype(jnp.int32).reshape(1)
    core = lax.axis_index("core").astype(jnp.int32).reshape(1)
    pred, normed = forward(fields, weight, bias.reshape(1, V), gain_row)
    pred = swap(pred, MEMBER)
    resid = residual(fields, gain_row, normed)
    pred, resid = lax.optimization_barrier((pred, resid))
    grad, loss = pair(slot, pred, observed, lat, vw_row)
    grad = swap(grad, MEMBER)
    sums = weight_part(grad, weight, gain_row, lat, loss, normed, resid)
    sums = lax.all_gather(sums, "core")
    sums = fold(core, sums)
    sums = swap(sums.reshape(CHIPS, 2, LANES), CHIP)
    sums, lat_total = share(sums.reshape(D // 2, LANES))
    sums = swap(sums.reshape(CHIPS, 2, LANES), CHIP)
    grad_fields = fields_part(fields, grad, weight, gain_row, lat_total, points_total)
    sums = lax.all_gather(sums.reshape(D // 2, LANES), "core", tiled=True)
    grad_weight, grad_gain, grad_bias, loss = finish(sums, points_total)
    return (
        grad_fields.reshape(1, LOCAL, D),
        grad_weight,
        grad_gain.reshape(D),
        grad_bias.reshape(V),
        loss.reshape(()),
    )


def solution(mesh):
    devices = mesh.devices.reshape(4, 2, 8, 4, 2)
    fine = Mesh(devices, ("x", "y_lo", "z", "y_hi", "core"))
    points_total = float(LOCAL * mesh.shape["grid"])
    return jax.shard_map(
        functools.partial(shards, points_total),
        mesh=fine,
        in_specs=(P(MEMBER, GRID, None), P(None, GRID), P(GRID), P(), P(), P(), P()),
        out_specs=(P(MEMBER, GRID, None), P(), P(), P(), P()),
        check_vma=False,
    )
```

time: 123 us -> 118 us (0.959)
  blocking collectives: 69 us -> 58.2 us
  Pallas kernels: 10.4 us -> 21.1 us
  local copies, waits for them, and re-layouts: 7.56 us -> 0.04 us
  starting transfers between devices: 17.1 us -> 20.1 us
    all_to_all x4 -> x2, blocking collectives: 69 us -> 47.9 us  [swap(): return lax.all_to_all(array, axes, split_axis=0, concat_axis=0, tiled=True)]
    pallas_call x7, Pallas kernels: 6.7 us -> 17.3 us  [the longest x1 4.98 us: residual(): pl.pallas_call(residual_kernel, grid=(LOCAL // TILE,), in_specs=[block, p...]
    all_gather x0 -> x2, blocking collectives: none -> 10.3 us  [the longest x1 5.43 us: shards(): sums = lax.all_gather(sums, 'core')]
    unnamed x26 -> x16, local copies, waits for them, and re-layouts: 7.56 us -> 0.04 us
    all_to_all x2, starting transfers between devices: 17.1 us -> 20.1 us  [swap(): return lax.all_to_all(array, axes, split_axis=0, concat_axis=0, tiled=True)]
  transfers between devices with their start and end apart: 2 -> 2, of which waited for: 2 -> 2; matrix products, arithmetic and copies ran while one was open for 0% -> 0% of each run, Pallas kernels for 3% -> 7%
where the time goes in v2:
time: 118 us
  blocking collectives  58.2 us (49%)
  Pallas kernels  21.1 us (18%)
  starting transfers between devices  20.1 us (17%)
  waiting for transfers between devices  17.4 us (15%)
    all_to_all x2, blocking collectives, swap(): return lax.all_to_all(array, axes, split_axis=0, concat_axis=0, tiled=True)  47.9 us
    all_to_all x2, starting transfers between devices, swap(): return lax.all_to_all(array, axes, split_axis=0, concat_axis=0, tiled=True)  20.1 us
    all_to_all x2, waiting for transfers between devices, swap(): return lax.all_to_all(array, axes, split_axis=0, concat_axis=0, tiled=True)  17.4 us
    all_gather x1, blocking collectives, shards(): sums = lax.all_gather(sums, 'core')  5.43 us
    pallas_call x1, Pallas kernels, residual(): pl.pallas_call(residual_kernel, grid=(LOCAL // TILE,), in_specs=[block, p...  4.98 us
    pallas_call x1, Pallas kernels, weight_part(): pl.pallas_call(weight_kernel, in_specs=[HBM] * 7, out_specs=VMEM, out_sha...  4.92 us
    all_gather x1, blocking collectives, shards(): sums = lax.all_gather(sums.reshape(D // 2, LANES), 'core', tiled=True)  4.87 us
    pallas_call x1, Pallas kernels, forward(): pl.pallas_call(forward_kernel, in_specs=[HBM] * 4, out_specs=[HBM] * 2, o...  4.82 us
  transfers between devices with their start and end apart: 2, of which 2 were waited for; matrix products, arithmetic and copies ran while one was open for 0% of the time, Pallas kernels for 7%

profile of v2, /device:TPU:1, one launch (start us, length us, event | category | flops | bytes accessed | tf_op | source)
XLA Modules:
  0.0 117.6 jit_solution(757645053021424647)
XLA Ops:
  0.6 4.8 %shard_map.110 = (f32[8,100,128]{2,1,0:T(8,128)}, bf16[1024,1024]{1,0:T(8,128)(2,1)}) custom-call(bf16[1024,1024]{1,0:T(8,128)(2,1)} %bitcast.16, bf16[100,1024]{1,0:T(8,128)(2,1)} %weight_ref.1, f32[1,100]{1,0:T(1,128)} %bitcast.31, f32[1,1024]{1,0:T(1,128)} %bitcast.22), custom_call_target="tpu_custom_call" | custom-call | flops 209715200 | bytes 6291456 | tf_op jit(solution)/shard_map/pallas_call | solution.py:96
  5.5 10.3 %all-to-all-start = ((f32[8,100,128]{2,1,0:T(8,128)}), f32[8,100,128]{2,1,0:T(8,128)S(1)}, u32[]{:S(2)}, u32[]{:S(2)}) async-start(f32[8,100,128]{2,1,0:T(8,128)} %get-tuple-element.17), calls=%async_computation | async-start | bytes 851968 | tf_op jit(solution)/shard_map/all_to_all | solution.py:369
  15.7 0.0 copy-start.3
  15.7 0.0 copy-start.5
  15.7 0.0 copy-start.7
  15.7 5.0 %shard_map.111.resid_hbm = bf16[1024,1024]{1,0:T(8,128)(2,1)} custom-call(bf16[1024,1024]{1,0:T(8,128)(2,1)} %bitcast.17, f32[1,1024]{1,0:T(1,128)} %bitcast.23, bf16[1024,1024]{1,0:T(8,128)(2,1)} %get-tuple-element.18.normed_ref.normed_hbm), custom_call_target="tpu_custom_call" | custom-call | flops 12582912 | bytes 6291456 | tf_op jit(solution)/shard_map/pallas_call | solution.py:126
  20.7 8.3 %all-to-all-done.pred_ref = f32[8,100,128]{2,1,0:T(8,128)S(1)} async-done(((f32[8,100,128]{2,1,0:T(8,128)}), f32[8,100,128]{2,1,0:T(8,128)S(1)}, u32[]{:S(2)}, u32[]{:S(2)}) %all-to-all-start) | async-done | bytes 409632 | tf_op jit(solution)/shard_map/all_to_all | solution.py:369
  29.0 0.0 copy-done.3
  29.0 0.0 copy-done.5
  29.0 0.0 copy-done.7
  29.0 0.6 shard_map.112
  29.6 0.0 copy-start.6
  29.6 16.9 %all_to_all.20.grad_hbm.grad_ref = f32[8,100,128]{2,1,0:T(8,128)} all-to-all(f32[8,100,128]{2,1,0:T(8,128)S(1)} %get-tuple-element.20), channel_id=1, replica_groups=mesh['x'=4,'y_lo'=2,'z'=8,'y_hi'=4,'core'=2] {'y_hi','core'}, dimensions={0} | all-to-all | bytes 819200 | tf_op jit(solution)/shard_map/all_to_all | solution.py:369
  46.5 0.0 copy-done.6
  46.5 4.9 %shard_map.113 = f32[104,1024]{1,0:T(8,128)} custom-call(f32[8,100,128]{2,1,0:T(8,128)} %all_to_all.20.grad_hbm.grad_ref, bf16[100,1024]{1,0:T(8,128)(2,1)} %weight_ref.1, f32[1,1024]{1,0:T(1,128)} %bitcast.24, f32[8,128]{1,0:T(8,128)} %bitcast.26, f32[8,128]{1,0:T(8,128)} %copy-done.6, bf16[1024,1024]{1,0:T(8,128)(2,1)} %get-tuple-element.18.normed_ref.normed_hbm, ...), custom_call_target="tpu_custom_call" | custom-call | flops 419430400 | bytes 4194304 | tf_op jit(solution)/shard_map/pallas_call | solution.py:248
  51.5 0.0 copy-start
  51.5 0.0 copy-start.1
  51.5 0.0 copy-start.2
  51.5 0.0 copy-start.4
  51.5 5.4 %all-gather = f32[208,1024]{1,0:T(8,128)S(1)} all-gather(f32[104,1024]{1,0:T(8,128)} %shard_map.113), channel_id=2, replica_groups=mesh['x'=4,'y_lo'=2,'z'=8,'y_hi'=4,'core'=2] {'core'}, dimensions={0}, use_global_device_ids=true | all-gather | bytes 1277952 | tf_op jit(solution)/shard_map/all_gather | solution.py:386
  56.9 0.1 shard_map.114
  57.1 31.0 %all_to_all.21 = f32[256,2,128]{2,1,0:T(2,128)S(1)} all-to-all(f32[256,2,128]{2,1,0:T(2,128)S(1)} %bitcast.21), channel_id=1, replica_groups=mesh['x'=4,'y_lo'=2,'z'=8,'y_hi'=4,'core'=2] {'x','y_lo','z','y_hi'}, dimensions={0} | all-to-all | bytes 524288 | tf_op jit(solution)/shard_map/all_to_all | solution.py:369
  88.1 0.8 shard_map.115
  88.9 9.9 %all-to-all-start.3 = ((f32[256,2,128]{2,1,0:T(2,128)}), f32[256,2,128]{2,1,0:T(2,128)S(1)}, u32[]{:S(2)}, u32[]{:S(2)}) async-start(f32[256,2,128]{2,1,0:T(2,128)} %bitcast.11), calls=%async_computation.3 | async-start | bytes 524288 | tf_op jit(solution)/shard_map/all_to_all | solution.py:369
  98.7 0.0 copy-done
  98.7 0.0 copy-done.1
  98.7 0.0 copy-done.2
  98.8 0.0 copy-done.4
  98.8 3.8 %shard_map.116 = bf16[1024,1024]{1,0:T(8,128)(2,1)} custom-call(bf16[1024,1024]{1,0:T(8,128)(2,1)S(1)} %bitcast.18, f32[8,100,128]{2,1,0:T(8,128)S(1)} %copy-done.1, bf16[100,1024]{1,0:T(8,128)(2,1)S(1)} %copy-done.2, f32[1,1024]{1,0:T(1,128)S(1)} %bitcast.25, f32[8,128]{1,0:T(8,128)S(1)} %get-tuple-element.23.lat_ref), custom_call_target="tpu_custom_call" | custom-call | flops 209715200 | bytes 12582912 | tf_op jit(solution)/shard_map/pallas_call | solution.py:351
  102.5 9.1 %all-to-all-done.3 = f32[256,2,128]{2,1,0:T(2,128)S(1)} async-done(((f32[256,2,128]{2,1,0:T(2,128)}), f32[256,2,128]{2,1,0:T(2,128)S(1)}, u32[]{:S(2)}, u32[]{:S(2)}) %all-to-all-start.3) | async-done | bytes 262176 | tf_op jit(solution)/shard_map/all_to_all | solution.py:369
  111.6 4.9 %all_gather.11.parts_ref = f32[1024,128]{1,0:T(8,128)S(1)} all-gather(f32[512,128]{1,0:T(8,128)S(1)} %bitcast.30), channel_id=1, replica_groups=mesh['x'=4,'y_lo'=2,'z'=8,'y_hi'=4,'core'=2] {'core'}, dimensions={0}, use_global_device_ids=true | all-gather | bytes 786432 | tf_op jit(solution)/shard_map/all_gather | solution.py:392
  116.5 1.1 shard_map.117
Async XLA Ops:
  5.5 23.6 %all-to-all-start = ((f32[8,100,128]{2,1,0:T(8,128)}), f32[8,100,128]{2,1,0:T(8,128)S(1)}, u32[]{:S(2)}, u32[]{:S(2)}) async-start(f32[8,100,128]{2,1,0:T(8,128)} %get-tuple-element.17), calls=%async_computation | async-start | bytes 851968 | tf_op jit(solution)/shard_map/all_to_all | solution.py:369
  15.7 13.3 %copy-start.3 = (bf16[100,1024]{1,0:T(8,128)(2,1)S(1)}, bf16[100,1024]{1,0:T(8,128)(2,1)}, u32[]{:S(2)}) copy-start(bf16[100,1024]{1,0:T(8,128)(2,1)} %obs_ref.1) | copy-start | bytes 614404
  15.7 13.3 %copy-start.5 = (f32[1024]{0:T(1024)S(1)}, f32[1024]{0:T(1024)}, u32[]{:S(2)}) copy-start(f32[1024]{0:T(1024)} %param.9) | copy-start | bytes 12292
  15.7 13.3 %copy-start.7 = (f32[100]{0:T(128)S(1)}, f32[100]{0:T(128)}, u32[]{:S(2)}) copy-start(f32[100]{0:T(128)} %param.10) | copy-start | bytes 1204
  29.6 16.9 %copy-start.6 = (f32[8,128]{1,0:T(8,128)}, f32[8,128]{1,0:T(8,128)S(1)}, u32[]{:S(2)}) copy-start(f32[8,128]{1,0:T(8,128)S(1)} %get-tuple-element.21.loss_hbm) | copy-start | bytes 12292
  51.5 47.3 %copy-start = (bf16[1,1024,1024]{2,1,0:T(8,128)(2,1)S(1)}, bf16[1,1024,1024]{2,1,0:T(8,128)(2,1)}, u32[]{:S(2)}) copy-start(bf16[1,1024,1024]{2,1,0:T(8,128)(2,1)} %param.7) | copy-start | bytes 6291460
  51.5 47.3 %copy-start.1 = (f32[8,100,128]{2,1,0:T(8,128)S(1)}, f32[8,100,128]{2,1,0:T(8,128)}, u32[]{:S(2)}) copy-start(f32[8,100,128]{2,1,0:T(8,128)} %all_to_all.20.grad_hbm.grad_ref) | copy-start | bytes 1228804
  51.5 47.3 %copy-start.2 = (bf16[100,1024]{1,0:T(8,128)(2,1)S(1)}, bf16[100,1024]{1,0:T(8,128)(2,1)}, u32[]{:S(2)}) copy-start(bf16[100,1024]{1,0:T(8,128)(2,1)} %weight_ref.1) | copy-start | bytes 614404
  51.5 47.3 %copy-start.4 = (f32[1024]{0:T(1024)S(1)}, f32[1024]{0:T(1024)}, u32[]{:S(2)}) copy-start(f32[1024]{0:T(1024)} %param.13) | copy-start | bytes 12292
  88.9 22.7 %all-to-all-start.3 = ((f32[256,2,128]{2,1,0:T(2,128)}), f32[256,2,128]{2,1,0:T(2,128)S(1)}, u32[]{:S(2)}, u32[]{:S(2)}) async-start(f32[256,2,128]{2,1,0:T(2,128)} %bitcast.11), calls=%async_computation.3 | async-start | bytes 524288 | tf_op jit(solution)/shard_map/all_to_all | solution.py:369

commit v3 on v2

--- a/solution.py
+++ b/solution.py
@@ -22,8 +22,9 @@
 MEMBER = ("y_hi", "core")
 CHIP = ("x", "y_lo", "z", "y_hi")
 VMEM_LIMIT = 16 * 1024 * 1024
-WHOLE_VMEM = 60 * 1024 * 1024
-RESIDUAL_VMEM = 62 * 1024 * 1024
+FORWARD_VMEM = 60 * 1024 * 1024
+RESIDUAL_VMEM = 60 * 1024 * 1024
+WEIGHT_VMEM = 50 * 1024 * 1024
 VMEM = pl.BlockSpec(memory_space=pltpu.VMEM)
 SMEM = pl.BlockSpec(memory_space=pltpu.SMEM)
 HBM = pl.BlockSpec(memory_space=pltpu.HBM)
@@ -52,17 +53,15 @@
 
 def forward_kernel(fields_hbm, weight_hbm, bias_hbm, gain_hbm, pred_hbm, normed_hbm,
                    fields_ref, weight_ref, bias_ref, gain_ref, pred_ref, normed_ref, in_sems, out_sems):
-    tiles = LOCAL // TILE
-    slots = TILE // LANES
-    rows = [pl.ds(t * TILE, TILE) for t in range(tiles)]
+    rows = [pl.ds(t * LANES, LANES) for t in range(M)]
     small = [
-        pltpu.make_async_copy(gain_hbm, gain_ref, in_sems.at[tiles]),
-        pltpu.make_async_copy(weight_hbm, weight_ref, in_sems.at[tiles + 1]),
-        pltpu.make_async_copy(bias_hbm, bias_ref, in_sems.at[tiles + 2]),
+        pltpu.make_async_copy(gain_hbm, gain_ref, in_sems.at[M]),
+        pltpu.make_async_copy(weight_hbm, weight_ref, in_sems.at[M + 1]),
+        pltpu.make_async_copy(bias_hbm, bias_ref, in_sems.at[M + 2]),
     ]
     large = [
         pltpu.make_async_copy(fields_hbm.at[rows[t]], fields_ref.at[rows[t]], in_sems.at[t])
-        for t in range(tiles)
+        for t in range(M)
     ]
     large[0].start()
     for copy in small:
@@ -70,33 +69,30 @@
     for copy in large[1:]:
         copy.start()
     back = []
-    for t in range(tiles):
+    for t in range(M):
         large[t].wait()
+        unit, _ = unit_of(fields_ref[rows[t]].astype(f32))
         if t == 0:
             for copy in small:
                 copy.wait()
             bias = column(bias_ref[...])[:V]
-        unit, _ = unit_of(fields_ref[rows[t]].astype(f32))
         normed = (unit * gain_ref[...]).astype(bf16)
         normed_ref[rows[t]] = normed
+        back.append(pltpu.make_async_copy(normed_ref.at[rows[t]], normed_hbm.at[rows[t]], out_sems.at[t, 1]))
+        back[-1].start()
         pred = lax.dot_general(weight_ref[...], normed, NT, preferred_element_type=f32)
-        for k in range(slots):
-            pred_ref[t * slots + k] = pred[:, k * LANES : (k + 1) * LANES] + bias
-        here = pl.ds(t * slots, slots)
-        back.append(pltpu.make_async_copy(pred_ref.at[here], pred_hbm.at[here], out_sems.at[t, 0]))
-        back.append(pltpu.make_async_copy(normed_ref.at[rows[t]], normed_hbm.at[rows[t]], out_sems.at[t, 1]))
-        back[-2].start()
+        pred_ref[t] = pred + bias
+        back.append(pltpu.make_async_copy(pred_ref.at[t], pred_hbm.at[t], out_sems.at[t, 0]))
         back[-1].start()
     for copy in back:
         copy.wait()
 
 
 def forward(fields, weight, bias, gain):
-    tiles = LOCAL // TILE
     return pl.pallas_call(
         forward_kernel,
         in_specs=[HBM] * 4,
-        out_specs=[HBM] * 2,
+        out_specs=[HBM, HBM],
         out_shape=[
             jax.ShapeDtypeStruct((M, V, LANES), f32),
             jax.ShapeDtypeStruct((LOCAL, D), bf16),
@@ -108,10 +104,10 @@
             pltpu.VMEM((1, D), f32),
             pltpu.VMEM((M, V, LANES), f32),
             pltpu.VMEM((LOCAL, D), bf16),
-            pltpu.SemaphoreType.DMA((tiles + 3,)),
-            pltpu.SemaphoreType.DMA((tiles, 2)),
-        ],
-        compiler_params=params(WHOLE_VMEM),
+            pltpu.SemaphoreType.DMA((M + 3,)),
+            pltpu.SemaphoreType.DMA((M, 2)),
+        ],
+        compiler_params=params(FORWARD_VMEM),
         cost_estimate=pl.CostEstimate(flops=2 * V * D * LOCAL, bytes_accessed=6 << 20, transcendentals=0),
     )(fields, weight, bias, gain)
 
@@ -192,76 +188,46 @@
     )(slot, pred, observed, lat, var_weight)
 
 
-def weight_kernel(grad_hbm, weight_hbm, gain_hbm, lat_hbm, loss_hbm, normed_hbm, resid_hbm, out_ref,
-                  grad_ref, weight_ref, gain_ref, lat_ref, loss_ref, normed_ref, resid_ref, small_sems, sems):
+def weight_kernel(grad_ref, weight_ref, gain_ref, lat_ref, loss_ref, normed_ref, resid_hbm, out_ref, resid_ref, sems):
     tiles = LOCAL // TILE
-    slots = TILE // LANES
-    small = [
-        pltpu.make_async_copy(grad_hbm, grad_ref, small_sems.at[0]),
-        pltpu.make_async_copy(loss_hbm, loss_ref, small_sems.at[1]),
-        pltpu.make_async_copy(lat_hbm, lat_ref, small_sems.at[2]),
-        pltpu.make_async_copy(weight_hbm, weight_ref, small_sems.at[3]),
-        pltpu.make_async_copy(gain_hbm, gain_ref, small_sems.at[4]),
-    ]
-    for copy in small:
-        copy.start()
-    copies = []
-    for t in range(tiles):
-        rows = pl.ds(t * TILE, TILE)
-        copies.append((
-            pltpu.make_async_copy(normed_hbm.at[rows], normed_ref.at[rows], sems.at[t, 0]),
-            pltpu.make_async_copy(resid_hbm.at[rows], resid_ref.at[rows], sems.at[t, 1]),
-        ))
-    for copy, _ in copies:
-        copy.start()
-    for _, copy in copies:
-        copy.start()
-    for copy in small:
-        copy.wait()
-    grads = [
-        jnp.concatenate([grad_ref[t * slots + k] for k in range(slots)], axis=1).astype(bf16)
+    copies = [
+        pltpu.make_async_copy(
+            resid_hbm.at[pl.ds(t * TILE, TILE)], resid_ref.at[pl.ds(t * TILE, TILE)], sems.at[t]
+        )
         for t in range(tiles)
     ]
+    for copy in copies:
+        copy.start()
+    grad = jnp.concatenate([grad_ref[k] for k in range(M)], axis=1).astype(bf16)
     ones = jnp.ones((8, LOCAL), bf16)
-    sums = lax.dot_general(ones, jnp.concatenate(grads, axis=1), NT, preferred_element_type=f32)
+    sums = lax.dot_general(ones, grad, NT, preferred_element_type=f32)
     loss = jnp.sum(loss_ref[...], keepdims=True)
     lane = lax.broadcasted_iota(jnp.int32, (1, D), 1)
     misc = jnp.concatenate([sums[0:1], jnp.zeros((1, D - V), f32)], axis=1)
     misc = jnp.where(lane == V, loss, misc)
     lat = jnp.broadcast_to(jnp.sum(lat_ref[...], keepdims=True), (1, D))
-    total = jnp.zeros((V, D), f32)
-    for t in range(tiles):
-        copies[t][0].wait()
-        rows = pl.ds(t * TILE, TILE)
-        total = total + jnp.dot(grads[t], normed_ref[rows], preferred_element_type=f32)
+    out_ref[:V] = jnp.dot(grad, normed_ref[...], preferred_element_type=f32)
     rest = jnp.zeros((V, D), f32)
     for t in range(tiles):
-        copies[t][1].wait()
-        rows = pl.ds(t * TILE, TILE)
-        rest = rest + jnp.dot(grads[t], resid_ref[rows], preferred_element_type=f32)
-    part_gain = jnp.sum(weight_ref[...].astype(f32) * (total + rest), axis=0, keepdims=True) / gain_ref[...]
-    out_ref[:V] = total
+        copies[t].wait()
+        rows = slice(t * TILE, (t + 1) * TILE)
+        rest = rest + jnp.dot(grad[:, rows], resid_ref[rows], preferred_element_type=f32)
+    part_gain = weight_ref[...].astype(f32) * (out_ref[:V] + rest)
+    part_gain = jnp.sum(part_gain, axis=0, keepdims=True) / gain_ref[...]
     out_ref[V:] = jnp.concatenate([part_gain, misc, lat, jnp.zeros((1, D), f32)], axis=0)
 
 
 def weight_part(grad, weight, gain, lat, loss, normed, resid):
     return pl.pallas_call(
         weight_kernel,
-        in_specs=[HBM] * 7,
+        in_specs=[VMEM] * 6 + [HBM],
         out_specs=VMEM,
         out_shape=jax.ShapeDtypeStruct((ROWS, D), f32),
         scratch_shapes=[
-            pltpu.VMEM((M, V, LANES), f32),
-            pltpu.VMEM((V, D), bf16),
-            pltpu.VMEM((1, D), f32),
-            pltpu.VMEM((M, LANES), f32),
-            pltpu.VMEM((8, LANES), f32),
             pltpu.VMEM((LOCAL, D), bf16),
-            pltpu.VMEM((LOCAL, D), bf16),
-            pltpu.SemaphoreType.DMA((5,)),
-            pltpu.SemaphoreType.DMA((LOCAL // TILE, 2)),
-        ],
-        compiler_params=params(WHOLE_VMEM),
+            pltpu.SemaphoreType.DMA((LOCAL // TILE,)),
+        ],
+        compiler_params=params(WEIGHT_VMEM),
         cost_estimate=pl.CostEstimate(flops=4 * V * D * LOCAL, bytes_accessed=4 << 20, transcendentals=0),
     )(grad, weight, gain, lat, loss, normed, resid)
 

time: 118 us -> 115 us (0.975)
  Pallas kernels: 21.1 us -> 19.4 us
    pallas_call x2, Pallas kernels: 9.74 us -> 8.01 us  [the longest x1 5.77 us: forward(): pl.pallas_call(forward_kernel, in_specs=[HBM] * 4, out_specs=[HBM, HBM],...]
  transfers between devices with their start and end apart: 2 -> 2, of which waited for: 2 -> 2; matrix products, arithmetic and copies ran while one was open for 0% -> 0% of each run, Pallas kernels for 7% -> 8%
where the time goes in v3:
time: 115 us
  blocking collectives  57.3 us (50%)
  starting transfers between devices  20.1 us (17%)
  Pallas kernels  19.4 us (17%)
  waiting for transfers between devices  17.3 us (15%)
    all_to_all x2, blocking collectives, swap(): return lax.all_to_all(array, axes, split_axis=0, concat_axis=0, tiled=True)  47.2 us
    all_to_all x2, starting transfers between devices, swap(): return lax.all_to_all(array, axes, split_axis=0, concat_axis=0, tiled=True)  20.1 us
    all_to_all x2, waiting for transfers between devices, swap(): return lax.all_to_all(array, axes, split_axis=0, concat_axis=0, tiled=True)  17.3 us
    pallas_call x1, Pallas kernels, forward(): pl.pallas_call(forward_kernel, in_specs=[HBM] * 4, out_specs=[HBM, HBM],...  5.77 us
    all_gather x1, blocking collectives, shards(): sums = lax.all_gather(sums, 'core')  5.21 us
    pallas_call x1, Pallas kernels, residual(): pl.pallas_call(residual_kernel, grid=(LOCAL // TILE,), in_specs=[block, p...  5.07 us
    all_gather x1, blocking collectives, shards(): sums = lax.all_gather(sums.reshape(D // 2, LANES), 'core', tiled=True)  4.87 us
    pallas_call x1, Pallas kernels, fields_part(): pl.pallas_call(functools.partial(fields_kernel, points_total), grid=(LOCA...  3.77 us
  transfers between devices with their start and end apart: 2, of which 2 were waited for; matrix products, arithmetic and copies ran while one was open for 0% of the time, Pallas kernels for 8%

profile of v3, /device:TPU:1, one launch (start us, length us, event | category | flops | bytes accessed | tf_op | source)
XLA Modules:
  0.0 114.9 jit_solution(9277317213437903704)
XLA Ops:
  0.6 5.8 %shard_map.110 = (f32[8,100,128]{2,1,0:T(8,128)}, bf16[1024,1024]{1,0:T(8,128)(2,1)}) custom-call(bf16[1024,1024]{1,0:T(8,128)(2,1)} %bitcast.16, bf16[100,1024]{1,0:T(8,128)(2,1)} %weight_ref.3, f32[1,100]{1,0:T(1,128)} %bitcast.31, f32[1,1024]{1,0:T(1,128)} %bitcast.22), custom_call_target="tpu_custom_call" | custom-call | flops 209715200 | bytes 6291456 | tf_op jit(solution)/shard_map/pallas_call | solution.py:92
  6.4 10.3 %all-to-all-start = ((f32[8,100,128]{2,1,0:T(8,128)}), f32[8,100,128]{2,1,0:T(8,128)S(1)}, u32[]{:S(2)}, u32[]{:S(2)}) async-start(f32[8,100,128]{2,1,0:T(8,128)} %get-tuple-element.17), calls=%async_computation | async-start | bytes 851968 | tf_op jit(solution)/shard_map/all_to_all | solution.py:335
  16.7 0.0 copy-start.3
  16.7 0.0 copy-start.5
  16.7 0.0 copy-start.6
  16.7 0.0 copy-start.1
  16.7 0.0 copy-start.2
  16.7 0.0 copy-start.4
  16.7 5.1 %shard_map.111.resid_hbm = bf16[1024,1024]{1,0:T(8,128)(2,1)} custom-call(bf16[1024,1024]{1,0:T(8,128)(2,1)} %bitcast.17, f32[1,1024]{1,0:T(1,128)} %bitcast.23, bf16[1024,1024]{1,0:T(8,128)(2,1)} %get-tuple-element.18.normed_ref), custom_call_target="tpu_custom_call" | custom-call | flops 12582912 | bytes 6291456 | tf_op jit(solution)/shard_map/pallas_call | solution.py:122
  21.8 8.2 %all-to-all-done.pred_ref = f32[8,100,128]{2,1,0:T(8,128)S(1)} async-done(((f32[8,100,128]{2,1,0:T(8,128)}), f32[8,100,128]{2,1,0:T(8,128)S(1)}, u32[]{:S(2)}, u32[]{:S(2)}) %all-to-all-start) | async-done | bytes 409632 | tf_op jit(solution)/shard_map/all_to_all | solution.py:335
  30.0 0.0 copy-done.3
  30.0 0.0 copy-done.5
  30.0 0.0 copy-done.6
  30.0 0.6 shard_map.112
  30.6 16.2 %all_to_all.20.grad_ref = f32[8,100,128]{2,1,0:T(8,128)S(1)} all-to-all(f32[8,100,128]{2,1,0:T(8,128)S(1)} %get-tuple-element.20), channel_id=1, replica_groups=mesh['x'=4,'y_lo'=2,'z'=8,'y_hi'=4,'core'=2] {'y_hi','core'}, dimensions={0} | all-to-all | bytes 819200 | tf_op jit(solution)/shard_map/all_to_all | solution.py:335
  46.8 0.0 copy-done.1
  46.8 0.0 copy-done.2
  46.8 0.0 copy-done.4
  46.8 2.2 %shard_map.113 = f32[104,1024]{1,0:T(8,128)S(1)} custom-call(f32[8,100,128]{2,1,0:T(8,128)S(1)} %all_to_all.20.grad_ref, bf16[100,1024]{1,0:T(8,128)(2,1)S(1)} %copy-done.2, f32[1,1024]{1,0:T(1,128)S(1)} %bitcast.24, f32[8,128]{1,0:T(8,128)S(1)} %bitcast.27, f32[8,128]{1,0:T(8,128)S(1)} %get-tuple-element.21.loss_ref, bf16[1024,1024]{1,0:T(8,128)(2,1)S(1)} %copy-done.1, ...), custom_call_target="tpu_custom_call" | custom-call | flops 419430400 | bytes 4194304 | tf_op jit(solution)/shard_map/pallas_call | solution.py:221
  49.0 0.0 copy-start
  49.0 5.2 %all-gather = f32[208,1024]{1,0:T(8,128)S(1)} all-gather(f32[104,1024]{1,0:T(8,128)S(1)} %shard_map.113), channel_id=2, replica_groups=mesh['x'=4,'y_lo'=2,'z'=8,'y_hi'=4,'core'=2] {'core'}, dimensions={0}, use_global_device_ids=true | all-gather | bytes 1277952 | tf_op jit(solution)/shard_map/all_gather | solution.py:352
  54.3 0.1 shard_map.114
  54.4 31.0 %all_to_all.21 = f32[256,2,128]{2,1,0:T(2,128)S(1)} all-to-all(f32[256,2,128]{2,1,0:T(2,128)S(1)} %bitcast.21), channel_id=1, replica_groups=mesh['x'=4,'y_lo'=2,'z'=8,'y_hi'=4,'core'=2] {'x','y_lo','z','y_hi'}, dimensions={0} | all-to-all | bytes 524288 | tf_op jit(solution)/shard_map/all_to_all | solution.py:335
  85.4 0.8 shard_map.115
  86.2 9.9 %all-to-all-start.3 = ((f32[256,2,128]{2,1,0:T(2,128)}), f32[256,2,128]{2,1,0:T(2,128)S(1)}, u32[]{:S(2)}, u32[]{:S(2)}) async-start(f32[256,2,128]{2,1,0:T(2,128)} %bitcast.11), calls=%async_computation.3 | async-start | bytes 524288 | tf_op jit(solution)/shard_map/all_to_all | solution.py:335
  96.1 0.0 copy-done
  96.1 3.8 %shard_map.116 = bf16[1024,1024]{1,0:T(8,128)(2,1)} custom-call(bf16[1024,1024]{1,0:T(8,128)(2,1)S(1)} %bitcast.18, f32[8,100,128]{2,1,0:T(8,128)S(1)} %all_to_all.20.grad_ref, bf16[100,1024]{1,0:T(8,128)(2,1)S(1)} %copy-done.2, f32[1,1024]{1,0:T(1,128)S(1)} %bitcast.25, f32[8,128]{1,0:T(8,128)S(1)} %get-tuple-element.23.lat_ref), custom_call_target="tpu_custom_call" | custom-call | flops 209715200 | bytes 12582912 | tf_op jit(solution)/shard_map/pallas_call | solution.py:317
  99.8 9.1 %all-to-all-done.3 = f32[256,2,128]{2,1,0:T(2,128)S(1)} async-done(((f32[256,2,128]{2,1,0:T(2,128)}), f32[256,2,128]{2,1,0:T(2,128)S(1)}, u32[]{:S(2)}, u32[]{:S(2)}) %all-to-all-start.3) | async-done | bytes 262176 | tf_op jit(solution)/shard_map/all_to_all | solution.py:335
  108.9 4.9 %all_gather.11.parts_ref = f32[1024,128]{1,0:T(8,128)S(1)} all-gather(f32[512,128]{1,0:T(8,128)S(1)} %bitcast.30), channel_id=1, replica_groups=mesh['x'=4,'y_lo'=2,'z'=8,'y_hi'=4,'core'=2] {'core'}, dimensions={0}, use_global_device_ids=true | all-gather | bytes 786432 | tf_op jit(solution)/shard_map/all_gather | solution.py:358
  113.8 1.1 shard_map.117
Async XLA Ops:
  6.4 23.6 %all-to-all-start = ((f32[8,100,128]{2,1,0:T(8,128)}), f32[8,100,128]{2,1,0:T(8,128)S(1)}, u32[]{:S(2)}, u32[]{:S(2)}) async-start(f32[8,100,128]{2,1,0:T(8,128)} %get-tuple-element.17), calls=%async_computation | async-start | bytes 851968 | tf_op jit(solution)/shard_map/all_to_all | solution.py:335
  16.7 13.3 %copy-start.3 = (bf16[100,1024]{1,0:T(8,128)(2,1)S(1)}, bf16[100,1024]{1,0:T(8,128)(2,1)}, u32[]{:S(2)}) copy-start(bf16[100,1024]{1,0:T(8,128)(2,1)} %obs_ref.1) | copy-start | bytes 614404
  16.7 13.3 %copy-start.5 = (f32[1024]{0:T(1024)S(1)}, f32[1024]{0:T(1024)}, u32[]{:S(2)}) copy-start(f32[1024]{0:T(1024)} %param.9) | copy-start | bytes 12292
  16.7 13.3 %copy-start.6 = (f32[100]{0:T(128)S(1)}, f32[100]{0:T(128)}, u32[]{:S(2)}) copy-start(f32[100]{0:T(128)} %param.10) | copy-start | bytes 1204
  16.7 30.1 %copy-start.1 = (bf16[1024,1024]{1,0:T(8,128)(2,1)S(1)}, bf16[1024,1024]{1,0:T(8,128)(2,1)}, u32[]{:S(2)}) copy-start(bf16[1024,1024]{1,0:T(8,128)(2,1)} %get-tuple-element.18.normed_ref) | copy-start | bytes 6291460
  16.7 30.1 %copy-start.2 = (bf16[100,1024]{1,0:T(8,128)(2,1)S(1)}, bf16[100,1024]{1,0:T(8,128)(2,1)}, u32[]{:S(2)}) copy-start(bf16[100,1024]{1,0:T(8,128)(2,1)} %weight_ref.3) | copy-start | bytes 614404
  16.7 30.1 %copy-start.4 = (f32[1024]{0:T(1024)S(1)}, f32[1024]{0:T(1024)}, u32[]{:S(2)}) copy-start(f32[1024]{0:T(1024)} %param.13) | copy-start | bytes 12292
  49.0 47.0 %copy-start = (bf16[1,1024,1024]{2,1,0:T(8,128)(2,1)S(1)}, bf16[1,1024,1024]{2,1,0:T(8,128)(2,1)}, u32[]{:S(2)}) copy-start(bf16[1,1024,1024]{2,1,0:T(8,128)(2,1)} %param.7) | copy-start | bytes 6291460
  86.2 22.7 %all-to-all-start.3 = ((f32[256,2,128]{2,1,0:T(2,128)}), f32[256,2,128]{2,1,0:T(2,128)S(1)}, u32[]{:S(2)}, u32[]{:S(2)}) async-start(f32[256,2,128]{2,1,0:T(2,128)} %bitcast.11), calls=%async_computation.3 | async-start | bytes 524288 | tf_op jit(solution)/shard_map/all_to_all | solution.py:335

commit v4 on v3

--- a/solution.py
+++ b/solution.py
@@ -16,6 +16,9 @@
 CHIPS = 256
 LANES = 128
 TILE = 256
+BLOCK = 32
+PAIRS = 4
+PADDED = 104
 ROWS = 104
 GAIN_ROW, MISC_ROW, LAT_ROW = 100, 101, 102
 GRID = ("x", "y_lo", "z")
@@ -51,97 +54,106 @@
     return centred * inv_std, inv_std
 
 
-def forward_kernel(fields_hbm, weight_hbm, bias_hbm, gain_hbm, pred_hbm, normed_hbm,
+def scaled_rows(fields_ref, rows, gain):
+    unit, _ = unit_of(fields_ref[rows].astype(f32))
+    return unit * gain
+
+
+def forward_kernel(fields_hbm, weight_hbm, bias_hbm, gain_hbm, pred_hbm,
                    fields_ref, weight_ref, bias_ref, gain_ref, pred_ref, normed_ref, in_sems, out_sems):
-    rows = [pl.ds(t * LANES, LANES) for t in range(M)]
+    tiles = LOCAL // TILE
+    slots = TILE // LANES
+    rows = [pl.ds(t * TILE, TILE) for t in range(tiles)]
     small = [
-        pltpu.make_async_copy(gain_hbm, gain_ref, in_sems.at[M]),
-        pltpu.make_async_copy(weight_hbm, weight_ref, in_sems.at[M + 1]),
-        pltpu.make_async_copy(bias_hbm, bias_ref, in_sems.at[M + 2]),
+        pltpu.make_async_copy(gain_hbm, gain_ref, in_sems.at[tiles]),
+        pltpu.make_async_copy(weight_hbm, weight_ref, in_sems.at[tiles + 1]),
+        pltpu.make_async_copy(bias_hbm, bias_ref, in_sems.at[tiles + 2]),
     ]
     large = [
         pltpu.make_async_copy(fields_hbm.at[rows[t]], fields_ref.at[rows[t]], in_sems.at[t])
-        for t in range(M)
+        for t in range(tiles)
     ]
     large[0].start()
     for copy in small:
         copy.start()
     for copy in large[1:]:
         copy.start()
+    for copy in small:
+        copy.wait()
+    bias = column(bias_ref[...])[:V]
+    spare = jnp.zeros((PADDED - V, LANES), f32)
     back = []
-    for t in range(M):
+    for t in range(tiles):
         large[t].wait()
-        unit, _ = unit_of(fields_ref[rows[t]].astype(f32))
-        if t == 0:
-            for copy in small:
-                copy.wait()
-            bias = column(bias_ref[...])[:V]
-        normed = (unit * gain_ref[...]).astype(bf16)
-        normed_ref[rows[t]] = normed
-        back.append(pltpu.make_async_copy(normed_ref.at[rows[t]], normed_hbm.at[rows[t]], out_sems.at[t, 1]))
-        back[-1].start()
-        pred = lax.dot_general(weight_ref[...], normed, NT, preferred_element_type=f32)
-        pred_ref[t] = pred + bias
-        back.append(pltpu.make_async_copy(pred_ref.at[t], pred_hbm.at[t], out_sems.at[t, 0]))
+        for start in range(t * TILE, (t + 1) * TILE, BLOCK):
+            block = slice(start, start + BLOCK)
+            normed_ref[block] = scaled_rows(fields_ref, block, gain_ref[...]).astype(bf16)
+        pred = lax.dot_general(weight_ref[...], normed_ref[rows[t]], NT, preferred_element_type=f32)
+        for k in range(slots):
+            pred_ref[t * slots + k, :V] = pred[:, k * LANES : (k + 1) * LANES] + bias
+            pred_ref[t * slots + k, V:] = spare
+        here = pl.ds(t * slots, slots)
+        back.append(pltpu.make_async_copy(pred_ref.at[here], pred_hbm.at[here], out_sems.at[t]))
         back[-1].start()
     for copy in back:
         copy.wait()
 
 
 def forward(fields, weight, bias, gain):
+    tiles = LOCAL // TILE
     return pl.pallas_call(
         forward_kernel,
         in_specs=[HBM] * 4,
-        out_specs=[HBM, HBM],
-        out_shape=[
-            jax.ShapeDtypeStruct((M, V, LANES), f32),
-            jax.ShapeDtypeStruct((LOCAL, D), bf16),
-        ],
+        out_specs=HBM,
+        out_shape=jax.ShapeDtypeStruct((M, PADDED, LANES), f32),
         scratch_shapes=[
             pltpu.VMEM((LOCAL, D), bf16),
             pltpu.VMEM((V, D), bf16),
             pltpu.VMEM((1, V), f32),
             pltpu.VMEM((1, D), f32),
-            pltpu.VMEM((M, V, LANES), f32),
+            pltpu.VMEM((M, PADDED, LANES), f32),
             pltpu.VMEM((LOCAL, D), bf16),
-            pltpu.SemaphoreType.DMA((M + 3,)),
-            pltpu.SemaphoreType.DMA((M, 2)),
+            pltpu.SemaphoreType.DMA((tiles + 3,)),
+            pltpu.SemaphoreType.DMA((tiles,)),
         ],
         compiler_params=params(FORWARD_VMEM),
-        cost_estimate=pl.CostEstimate(flops=2 * V * D * LOCAL, bytes_accessed=6 << 20, transcendentals=0),
+        cost_estimate=pl.CostEstimate(flops=2 * V * D * LOCAL, bytes_accessed=3 << 20, transcendentals=0),
     )(fields, weight, bias, gain)
 
 
-def residual_kernel(fields_ref, gain_ref, normed_ref, out_ref):
-    unit, _ = unit_of(fields_ref[...].astype(f32))
-    out_ref[...] = (unit * gain_ref[...] - normed_ref[...].astype(f32)).astype(bf16)
-
-
-def residual(fields, gain, normed):
+def normed_kernel(fields_ref, gain_ref, normed_ref, resid_ref):
+    for start in range(0, TILE, BLOCK):
+        block = slice(start, start + BLOCK)
+        scaled = scaled_rows(fields_ref, block, gain_ref[...])
+        normed = scaled.astype(bf16)
+        normed_ref[block] = normed
+        resid_ref[block] = (scaled - normed.astype(f32)).astype(bf16)
+
+
+def normed_parts(fields, gain):
     block = pl.BlockSpec((TILE, D), lambda i: (i, 0))
     return pl.pallas_call(
-        residual_kernel,
+        normed_kernel,
         grid=(LOCAL // TILE,),
-        in_specs=[block, pl.BlockSpec((1, D), lambda i: (0, 0)), block],
-        out_specs=block,
-        out_shape=jax.ShapeDtypeStruct((LOCAL, D), bf16),
+        in_specs=[block, pl.BlockSpec((1, D), lambda i: (0, 0))],
+        out_specs=[block, block],
+        out_shape=[jax.ShapeDtypeStruct((LOCAL, D), bf16)] * 2,
         compiler_params=params(RESIDUAL_VMEM),
         cost_estimate=pl.CostEstimate(flops=12 * D * LOCAL, bytes_accessed=6 << 20, transcendentals=0),
-    )(fields, gain, normed)
-
-
-def pair_kernel(slot_ref, pred_ref, obs_ref, lat_ref, vw_ref, grad_ref, loss_ref):
-    count = pred_ref.shape[1]
+    )(fields, gain)
+
+
+def pair_kernel(slot_ref, core_ref, pred_ref, obs_ref, lat_ref, vw_ref, grad_ref, loss_ref):
     here = pl.ds(pl.multiple_of(slot_ref[0] * LANES, LANES), LANES)
     vw = column(vw_ref[...])
     observed = obs_ref[:, here].astype(f32)
     lat = lat_ref[pl.ds(slot_ref[0], 1), :]
     loss = jnp.zeros((8, LANES), f32)
-    for start in range(0, count, 8):
-        rows = min(8, count - start)
+    for start in range(0, V, 8):
+        rows = min(8, V - start)
         part = slice(start, start + rows)
         obs = observed[part]
-        pred = [pred_ref[m, part] for m in range(M)]
+        pred = [pred_ref[m % 2, m // 2, core_ref[0], part] for m in range(M)]
         sign = [None] * M
         pair_abs = None
         obs_abs = None
@@ -171,24 +183,26 @@
         scale = scale * (1.0 / (M * (M - 1)))
         for m in range(M):
             grad_ref[m, part] = sign[m] * scale
+    for m in range(M):
+        grad_ref[m, V:] = jnp.zeros((PADDED - V, LANES), f32)
     loss_ref[...] = loss
 
 
-def pair(slot, pred, observed, lat, var_weight):
+def pair(slot, core, pred, observed, lat, var_weight):
     return pl.pallas_call(
         pair_kernel,
-        in_specs=[SMEM] + [VMEM] * 4,
-        out_specs=[pl.BlockSpec(pred.shape, lambda: (0, 0, 0)), VMEM],
+        in_specs=[SMEM] * 2 + [VMEM] * 4,
+        out_specs=[VMEM] * 2,
         out_shape=[
-            jax.ShapeDtypeStruct(pred.shape, f32),
+            jax.ShapeDtypeStruct((M, PADDED, LANES), f32),
             jax.ShapeDtypeStruct((8, LANES), f32),
         ],
         compiler_params=params(),
         cost_estimate=pl.CostEstimate(flops=1 << 20, bytes_accessed=1 << 19, transcendentals=0),
-    )(slot, pred, observed, lat, var_weight)
-
-
-def weight_kernel(grad_ref, weight_ref, gain_ref, lat_ref, loss_ref, normed_ref, resid_hbm, out_ref, resid_ref, sems):
+    )(slot, core, pred, observed, lat, var_weight)
+
+
+def weight_kernel(core_ref, grad_ref, weight_ref, gain_ref, lat_ref, loss_ref, normed_ref, resid_hbm, out_ref, resid_ref, sems):
     tiles = LOCAL // TILE
     copies = [
         pltpu.make_async_copy(
@@ -198,7 +212,7 @@
     ]
     for copy in copies:
         copy.start()
-    grad = jnp.concatenate([grad_ref[k] for k in range(M)], axis=1).astype(bf16)
+    grad = jnp.concatenate([grad_ref[k % 2, k // 2, core_ref[0], :V] for k in range(M)], axis=1).astype(bf16)
     ones = jnp.ones((8, LOCAL), bf16)
     sums = lax.dot_general(ones, grad, NT, preferred_element_type=f32)
     loss = jnp.sum(loss_ref[...], keepdims=True)
@@ -217,10 +231,10 @@
     out_ref[V:] = jnp.concatenate([part_gain, misc, lat, jnp.zeros((1, D), f32)], axis=0)
 
 
-def weight_part(grad, weight, gain, lat, loss, normed, resid):
+def weight_part(core, grad, weight, gain, lat, loss, normed, resid):
     return pl.pallas_call(
         weight_kernel,
-        in_specs=[VMEM] * 6 + [HBM],
+        in_specs=[SMEM] + [VMEM] * 6 + [HBM],
         out_specs=VMEM,
         out_shape=jax.ShapeDtypeStruct((ROWS, D), f32),
         scratch_shapes=[
@@ -229,7 +243,7 @@
         ],
         compiler_params=params(WEIGHT_VMEM),
         cost_estimate=pl.CostEstimate(flops=4 * V * D * LOCAL, bytes_accessed=4 << 20, transcendentals=0),
-    )(grad, weight, gain, lat, loss, normed, resid)
+    )(core, grad, weight, gain, lat, loss, normed, resid)
 
 
 def fold_kernel(core_ref, parts_ref, out_ref):
@@ -300,10 +314,10 @@
     )(parts)
 
 
-def fields_kernel(points_total, fields_ref, grad_ref, weight_ref, gain_ref, lat_ref, out_ref):
+def fields_kernel(points_total, core_ref, fields_ref, grad_ref, weight_ref, gain_ref, lat_ref, out_ref):
+    del core_ref
     unit, inv_std = unit_of(fields_ref[...].astype(f32))
-    slots = grad_ref.shape[0]
-    grad = jnp.concatenate([grad_ref[k] for k in range(slots)], axis=1).astype(bf16)
+    grad = jnp.concatenate([grad_ref[0, 0, 0, :V], grad_ref[1, 0, 0, :V]], axis=1).astype(bf16)
     grad_normed = lax.dot_general(grad, weight_ref[...], TN, preferred_element_type=f32)
     grad_unit = grad_normed * gain_ref[...]
     mean_one = jnp.mean(grad_unit, axis=-1, keepdims=True)
@@ -312,27 +326,37 @@
     out_ref[...] = ((factor * inv_std) * (grad_unit - mean_one - unit * mean_two)).astype(bf16)
 
 
-def fields_part(fields, grad, weight, gain, lat_total, points_total):
-    slots = TILE // LANES
+def fields_part(core, fields, grad, weight, gain, lat_total, points_total):
     return pl.pallas_call(
         functools.partial(fields_kernel, points_total),
-        grid=(LOCAL // TILE,),
-        in_specs=[
-            pl.BlockSpec((TILE, D), lambda i: (i, 0)),
-            pl.BlockSpec((slots, V, LANES), lambda i: (i, 0, 0)),
-            pl.BlockSpec((V, D), lambda i: (0, 0)),
-            pl.BlockSpec((1, D), lambda i: (0, 0)),
-            pl.BlockSpec((8, LANES), lambda i: (0, 0)),
-        ],
-        out_specs=pl.BlockSpec((TILE, D), lambda i: (i, 0)),
+        grid_spec=pltpu.PrefetchScalarGridSpec(
+            num_scalar_prefetch=1,
+            grid=(PAIRS,),
+            in_specs=[
+                pl.BlockSpec((TILE, D), lambda i, c: (i, 0)),
+                pl.BlockSpec((2, 1, 1, PADDED, LANES), lambda i, c: (0, i, c[0], 0, 0)),
+                pl.BlockSpec((V, D), lambda i, c: (0, 0)),
+                pl.BlockSpec((1, D), lambda i, c: (0, 0)),
+                pl.BlockSpec((8, LANES), lambda i, c: (0, 0)),
+            ],
+            out_specs=pl.BlockSpec((TILE, D), lambda i, c: (i, 0)),
+        ),
         out_shape=jax.ShapeDtypeStruct((LOCAL, D), bf16),
         compiler_params=params(),
         cost_estimate=pl.CostEstimate(flops=2 * V * D * LOCAL, bytes_accessed=12 << 20, transcendentals=0),
-    )(fields, grad, weight, gain, lat_total)
+    )(core, fields, grad, weight, gain, lat_total)
 
 
 def swap(array, axes):
     return lax.all_to_all(array, axes, split_axis=0, concat_axis=0, tiled=True)
+
+
+def exchange(array):
+    return swap(array, "y_hi")
+
+
+def both_cores(array):
+    return lax.all_gather(array, "core").reshape(2, PAIRS, 2, PADDED, LANES)
 
 
 def shards(points_total, fields, observed, lat_weight, var_weight, weight, bias, gain):
@@ -342,19 +366,20 @@
     lat = lat_weight.reshape(M, LANES)
     slot = lax.axis_index(MEMBER).astype(jnp.int32).reshape(1)
     core = lax.axis_index("core").astype(jnp.int32).reshape(1)
-    pred, normed = forward(fields, weight, bias.reshape(1, V), gain_row)
-    pred = swap(pred, MEMBER)
-    resid = residual(fields, gain_row, normed)
-    pred, resid = lax.optimization_barrier((pred, resid))
-    grad, loss = pair(slot, pred, observed, lat, vw_row)
-    grad = swap(grad, MEMBER)
-    sums = weight_part(grad, weight, gain_row, lat, loss, normed, resid)
+    pred = forward(fields, weight, bias.reshape(1, V), gain_row)
+    pred = exchange(pred)
+    normed, resid = normed_parts(fields, gain_row)
+    pred, normed, resid = lax.optimization_barrier((pred, normed, resid))
+    pred = both_cores(pred)
+    grad, loss = pair(slot, core, pred, observed, lat, vw_row)
+    grad = both_cores(exchange(grad))
+    sums = weight_part(core, grad, weight, gain_row, lat, loss, normed, resid)
     sums = lax.all_gather(sums, "core")
     sums = fold(core, sums)
     sums = swap(sums.reshape(CHIPS, 2, LANES), CHIP)
     sums, lat_total = share(sums.reshape(D // 2, LANES))
     sums = swap(sums.reshape(CHIPS, 2, LANES), CHIP)
-    grad_fields = fields_part(fields, grad, weight, gain_row, lat_total, points_total)
+    grad_fields = fields_part(core, fields, grad, weight, gain_row, lat_total, points_total)
     sums = lax.all_gather(sums.reshape(D // 2, LANES), "core", tiled=True)
     grad_weight, grad_gain, grad_bias, loss = finish(sums, points_total)
     return (

time: 115 us -> 118 us (1.026)
  blocking collectives: 57.3 us -> 64.7 us
  starting transfers between devices: 20.1 us -> 17.6 us
  waiting for transfers between devices: 17.3 us -> 15.9 us
  Pallas kernels: 19.4 us -> 18.2 us
    all_gather x0 -> x2, blocking collectives: none -> 9.87 us  [both_cores(): return lax.all_gather(array, 'core').reshape(2, PAIRS, 2, PADDED, LANES)]
    all_gather x1, blocking collectives: 5.21 us -> 2.55 us  [shards(): sums = lax.all_gather(sums, 'core')]
    all_to_all x2, starting transfers between devices: 20.1 us -> 17.6 us  [swap(): return lax.all_to_all(array, axes, split_axis=0, concat_axis=0, tiled=True)]
    all_to_all x2, waiting for transfers between devices: 17.3 us -> 15.9 us  [swap(): return lax.all_to_all(array, axes, split_axis=0, concat_axis=0, tiled=True)]
    pallas_call x5, Pallas kernels: 17.4 us -> 16.2 us  [the longest x1 4.95 us: normed_parts(): pl.pallas_call(normed_kernel, grid=(LOCAL // TILE,), in_specs=[block, pl....]
  transfers between devices with their start and end apart: 2 -> 2, of which waited for: 2 -> 2; matrix products, arithmetic and copies ran while one was open for 0% -> 0% of each run, Pallas kernels for 8% -> 7%
where the time goes in v4:
time: 118 us; the launch traced here: 117 us
  blocking collectives  64.7 us (55%)
  Pallas kernels  18.2 us (15%)
  starting transfers between devices  17.6 us (15%)
  waiting for transfers between devices  15.9 us (13%)
    all_to_all x2, blocking collectives, swap(): return lax.all_to_all(array, axes, split_axis=0, concat_axis=0, tiled=True)  47.4 us
    all_to_all x2, starting transfers between devices, swap(): return lax.all_to_all(array, axes, split_axis=0, concat_axis=0, tiled=True)  17.6 us
    all_to_all x2, waiting for transfers between devices, swap(): return lax.all_to_all(array, axes, split_axis=0, concat_axis=0, tiled=True)  15.9 us
    all_gather x2, blocking collectives, both_cores(): return lax.all_gather(array, 'core').reshape(2, PAIRS, 2, PADDED, LANES)  9.87 us
    pallas_call x1, Pallas kernels, normed_parts(): pl.pallas_call(normed_kernel, grid=(LOCAL // TILE,), in_specs=[block, pl....  4.95 us
    all_gather x1, blocking collectives, shards(): sums = lax.all_gather(sums.reshape(D // 2, LANES), 'core', tiled=True)  4.87 us
    pallas_call x1, Pallas kernels, forward(): pl.pallas_call(forward_kernel, in_specs=[HBM] * 4, out_specs=HBM, out_sha...  4.66 us
    pallas_call x1, Pallas kernels, fields_part(): pl.pallas_call(functools.partial(fields_kernel, points_total), grid_spec=...  3.8 us
  transfers between devices with their start and end apart: 2, of which 2 were waited for; matrix products, arithmetic and copies ran while one was open for 0% of the time, Pallas kernels for 7%

profile of v4, /device:TPU:1, one launch (start us, length us, event | category | flops | bytes accessed | tf_op | source)
XLA Modules:
  0.0 117.2 jit_solution(14922809398525002935)
XLA Ops:
  0.6 4.7 %shard_map.110 = f32[8,104,128]{2,1,0:T(8,128)} custom-call(bf16[1024,1024]{1,0:T(8,128)(2,1)} %bitcast.18, bf16[100,1024]{1,0:T(8,128)(2,1)} %weight_ref.3, f32[1,100]{1,0:T(1,128)} %bitcast.36, f32[1,1024]{1,0:T(1,128)} %bitcast.27), custom_call_target="tpu_custom_call" | custom-call | flops 209715200 | bytes 3145728 | tf_op jit(solution)/shard_map/pallas_call | solution.py:104
  5.3 0.0 copy-start.3
  5.3 0.0 copy-start.5
  5.3 0.0 copy-start.6
  5.3 7.8 %all-to-all-start = ((f32[8,104,128]{2,1,0:T(8,128)}), f32[8,104,128]{2,1,0:T(8,128)S(1)}, u32[]{:S(2)}, u32[]{:S(2)}) async-start(f32[8,104,128]{2,1,0:T(8,128)} %shard_map.110), calls=%async_computation | async-start | bytes 851968 | tf_op jit(solution)/shard_map/all_to_all | solution.py:351
  13.1 5.0 %shard_map.111 = (bf16[1024,1024]{1,0:T(8,128)(2,1)}, bf16[1024,1024]{1,0:T(8,128)(2,1)}) custom-call(bf16[1024,1024]{1,0:T(8,128)(2,1)} %bitcast.19, f32[1,1024]{1,0:T(1,128)} %bitcast.28), custom_call_target="tpu_custom_call" | custom-call | flops 12582912 | bytes 6291456 | tf_op jit(solution)/shard_map/pallas_call | solution.py:135
  18.1 6.8 %all-to-all-done = f32[8,104,128]{2,1,0:T(8,128)S(1)} async-done(((f32[8,104,128]{2,1,0:T(8,128)}), f32[8,104,128]{2,1,0:T(8,128)S(1)}, u32[]{:S(2)}, u32[]{:S(2)}) %all-to-all-start) | async-done | bytes 426016 | tf_op jit(solution)/shard_map/all_to_all | solution.py:351
  24.9 0.0 copy-start.1
  24.9 0.0 copy-start.2
  24.9 0.0 copy-start.4
  24.9 5.0 %all-gather = f32[16,104,128]{2,1,0:T(8,128)S(1)} all-gather(f32[8,104,128]{2,1,0:T(8,128)S(1)} %all-to-all-done), channel_id=2, replica_groups=mesh['x'=4,'y_lo'=2,'z'=8,'y_hi'=4,'core'=2] {'core'}, dimensions={0}, use_global_device_ids=true | all-gather | bytes 1277952 | tf_op jit(solution)/shard_map/all_gather | solution.py:359
  29.9 0.0 copy-done.3
  29.9 0.0 copy-done.5
  29.9 0.0 copy-done.6
  29.9 0.6 shard_map.112
  30.5 15.7 %all_to_all.20 = f32[8,104,128]{2,1,0:T(8,128)S(1)} all-to-all(f32[8,104,128]{2,1,0:T(8,128)S(1)} %get-tuple-element.21), channel_id=1, replica_groups=mesh['x'=4,'y_lo'=2,'z'=8,'y_hi'=4,'core'=2] {'y_hi'}, dimensions={0} | all-to-all | bytes 851968 | tf_op jit(solution)/shard_map/all_to_all | solution.py:351
  46.2 4.9 %all-gather.1 = f32[16,104,128]{2,1,0:T(8,128)S(1)} all-gather(f32[8,104,128]{2,1,0:T(8,128)S(1)} %all_to_all.20), channel_id=3, replica_groups=mesh['x'=4,'y_lo'=2,'z'=8,'y_hi'=4,'core'=2] {'core'}, dimensions={0}, use_global_device_ids=true | all-gather | bytes 1277952 | tf_op jit(solution)/shard_map/all_gather | solution.py:359
  51.1 0.0 copy-done.1
  51.1 0.0 copy-done.2
  51.1 0.0 copy-done.4
  51.1 2.2 %shard_map.113 = f32[104,1024]{1,0:T(8,128)S(1)} custom-call(s32[1]{0:T(128)} %bitcast.core_ref, f32[2,4,2,104,128]{4,3,2,1,0:T(8,128)S(1)} %bitcast.21, bf16[100,1024]{1,0:T(8,128)(2,1)S(1)} %copy-done.2, f32[1,1024]{1,0:T(1,128)S(1)} %bitcast.29, f32[8,128]{1,0:T(8,128)S(1)} %bitcast.32, f32[8,128]{1,0:T(8,128)S(1)} %get-tuple-element.22.loss_ref, ...), custom_call_target="tpu_custom_call" | custom-call | flops 419430400 | bytes 4194304 | tf_op jit(solution)/shard_map/pallas_call | solution.py:235
  53.3 0.0 copy-start
  53.3 2.6 %all-gather.2 = f32[208,1024]{1,0:T(8,128)S(1)} all-gather(f32[104,1024]{1,0:T(8,128)S(1)} %shard_map.113), channel_id=4, replica_groups=mesh['x'=4,'y_lo'=2,'z'=8,'y_hi'=4,'core'=2] {'core'}, dimensions={0}, use_global_device_ids=true | all-gather | bytes 1277952 | tf_op jit(solution)/shard_map/all_gather | solution.py:377
  55.9 0.1 shard_map.114
  56.0 31.7 %all_to_all.21 = f32[256,2,128]{2,1,0:T(2,128)S(1)} all-to-all(f32[256,2,128]{2,1,0:T(2,128)S(1)} %bitcast.26), channel_id=1, replica_groups=mesh['x'=4,'y_lo'=2,'z'=8,'y_hi'=4,'core'=2] {'x','y_lo','z','y_hi'}, dimensions={0} | all-to-all | bytes 524288 | tf_op jit(solution)/shard_map/all_to_all | solution.py:351
  87.7 0.8 shard_map.115
  88.5 9.9 %all-to-all-start.3 = ((f32[256,2,128]{2,1,0:T(2,128)}), f32[256,2,128]{2,1,0:T(2,128)S(1)}, u32[]{:S(2)}, u32[]{:S(2)}) async-start(f32[256,2,128]{2,1,0:T(2,128)} %bitcast.13), calls=%async_computation.3 | async-start | bytes 524288 | tf_op jit(solution)/shard_map/all_to_all | solution.py:351
  98.4 0.0 copy-done
  98.4 3.8 %shard_map.116 = bf16[1024,1024]{1,0:T(8,128)(2,1)} custom-call(s32[1]{0:T(128)} %bitcast.core_ref, bf16[1024,1024]{1,0:T(8,128)(2,1)S(1)} %bitcast.20, f32[2,4,2,104,128]{4,3,2,1,0:T(8,128)S(1)} %bitcast.22, bf16[100,1024]{1,0:T(8,128)(2,1)S(1)} %copy-done.2, f32[1,1024]{1,0:T(1,128)S(1)} %bitcast.30, f32[8,128]{1,0:T(8,128)S(1)} %get-tuple-element.25.lat_ref), custom_call_target="tpu_custom_call" | custom-call | flops 209715200 | bytes 12582912 | tf_op jit(solution)/shard_map/pallas_call | solution.py:330
  102.2 9.1 %all-to-all-done.3 = f32[256,2,128]{2,1,0:T(2,128)S(1)} async-done(((f32[256,2,128]{2,1,0:T(2,128)}), f32[256,2,128]{2,1,0:T(2,128)S(1)}, u32[]{:S(2)}, u32[]{:S(2)}) %all-to-all-start.3) | async-done | bytes 262176 | tf_op jit(solution)/shard_map/all_to_all | solution.py:351
  111.2 4.9 %all_gather.27.parts_ref = f32[1024,128]{1,0:T(8,128)S(1)} all-gather(f32[512,128]{1,0:T(8,128)S(1)} %bitcast.35), channel_id=1, replica_groups=mesh['x'=4,'y_lo'=2,'z'=8,'y_hi'=4,'core'=2] {'core'}, dimensions={0}, use_global_device_ids=true | all-gather | bytes 786432 | tf_op jit(solution)/shard_map/all_gather | solution.py:383
  116.1 1.1 shard_map.117
Async XLA Ops:
  5.3 24.6 %copy-start.3 = (bf16[100,1024]{1,0:T(8,128)(2,1)S(1)}, bf16[100,1024]{1,0:T(8,128)(2,1)}, u32[]{:S(2)}) copy-start(bf16[100,1024]{1,0:T(8,128)(2,1)} %obs_ref.1) | copy-start | bytes 614404
  5.3 24.6 %copy-start.5 = (f32[1024]{0:T(1024)S(1)}, f32[1024]{0:T(1024)}, u32[]{:S(2)}) copy-start(f32[1024]{0:T(1024)} %param.9) | copy-start | bytes 12292
  5.3 24.6 %copy-start.6 = (f32[100]{0:T(128)S(1)}, f32[100]{0:T(128)}, u32[]{:S(2)}) copy-start(f32[100]{0:T(128)} %param.10) | copy-start | bytes 1204
  5.3 19.6 %all-to-all-start = ((f32[8,104,128]{2,1,0:T(8,128)}), f32[8,104,128]{2,1,0:T(8,128)S(1)}, u32[]{:S(2)}, u32[]{:S(2)}) async-start(f32[8,104,128]{2,1,0:T(8,128)} %shard_map.110), calls=%async_computation | async-start | bytes 851968 | tf_op jit(solution)/shard_map/all_to_all | solution.py:351
  24.9 26.2 %copy-start.1 = (bf16[1024,1024]{1,0:T(8,128)(2,1)S(1)}, bf16[1024,1024]{1,0:T(8,128)(2,1)}, u32[]{:S(2)}) copy-start(bf16[1024,1024]{1,0:T(8,128)(2,1)} %get-tuple-element.23.normed_ref) | copy-start | bytes 6291460
  24.9 26.2 %copy-start.2 = (bf16[100,1024]{1,0:T(8,128)(2,1)S(1)}, bf16[100,1024]{1,0:T(8,128)(2,1)}, u32[]{:S(2)}) copy-start(bf16[100,1024]{1,0:T(8,128)(2,1)} %weight_ref.3) | copy-start | bytes 614404
  24.9 26.2 %copy-start.4 = (f32[1024]{0:T(1024)S(1)}, f32[1024]{0:T(1024)}, u32[]{:S(2)}) copy-start(f32[1024]{0:T(1024)} %param.13) | copy-start | bytes 12292
  53.3 45.0 %copy-start = (bf16[1,1024,1024]{2,1,0:T(8,128)(2,1)S(1)}, bf16[1,1024,1024]{2,1,0:T(8,128)(2,1)}, u32[]{:S(2)}) copy-start(bf16[1,1024,1024]{2,1,0:T(8,128)(2,1)} %param.7) | copy-start | bytes 6291460
  88.5 22.7 %all-to-all-start.3 = ((f32[256,2,128]{2,1,0:T(2,128)}), f32[256,2,128]{2,1,0:T(2,128)S(1)}, u32[]{:S(2)}, u32[]{:S(2)}) async-start(f32[256,2,128]{2,1,0:T(2,128)} %bitcast.13), calls=%async_computation.3 | async-start | bytes 524288 | tf_op jit(solution)/shard_map/all_to_all | solution.py:351

commit v5 on v3

--- a/solution.py
+++ b/solution.py
@@ -16,11 +16,13 @@
 CHIPS = 256
 LANES = 128
 TILE = 256
+BLOCK = 32
 ROWS = 104
 GAIN_ROW, MISC_ROW, LAT_ROW = 100, 101, 102
 GRID = ("x", "y_lo", "z")
 MEMBER = ("y_hi", "core")
-CHIP = ("x", "y_lo", "z", "y_hi")
+PLACE = ("core", "y_hi")
+CHIP = ("x", "y_hi", "y_lo", "z")
 VMEM_LIMIT = 16 * 1024 * 1024
 FORWARD_VMEM = 60 * 1024 * 1024
 RESIDUAL_VMEM = 60 * 1024 * 1024
@@ -28,7 +30,8 @@
 VMEM = pl.BlockSpec(memory_space=pltpu.VMEM)
 SMEM = pl.BlockSpec(memory_space=pltpu.SMEM)
 HBM = pl.BlockSpec(memory_space=pltpu.HBM)
-f32, bf16 = jnp.float32, jnp.bfloat16
+f32, bf16, f8 = jnp.float32, jnp.bfloat16, jnp.float8_e4m3fn
+RESIDUAL_SCALE = 512.0
 NT = (((1,), (1,)), ((), ()))
 TN = (((0,), (0,)), ((), ()))
 
@@ -51,48 +54,61 @@
     return centred * inv_std, inv_std
 
 
+def scaled_rows(fields_ref, rows, gain):
+    unit, _ = unit_of(fields_ref[rows].astype(f32))
+    return unit * gain
+
+
 def forward_kernel(fields_hbm, weight_hbm, bias_hbm, gain_hbm, pred_hbm, normed_hbm,
                    fields_ref, weight_ref, bias_ref, gain_ref, pred_ref, normed_ref, in_sems, out_sems):
-    rows = [pl.ds(t * LANES, LANES) for t in range(M)]
+    tiles = LOCAL // TILE
+    slots = TILE // LANES
+    rows = [pl.ds(t * TILE, TILE) for t in range(tiles)]
     small = [
-        pltpu.make_async_copy(gain_hbm, gain_ref, in_sems.at[M]),
-        pltpu.make_async_copy(weight_hbm, weight_ref, in_sems.at[M + 1]),
-        pltpu.make_async_copy(bias_hbm, bias_ref, in_sems.at[M + 2]),
+        pltpu.make_async_copy(gain_hbm, gain_ref, in_sems.at[tiles]),
+        pltpu.make_async_copy(weight_hbm, weight_ref, in_sems.at[tiles + 1]),
+        pltpu.make_async_copy(bias_hbm, bias_ref, in_sems.at[tiles + 2]),
     ]
     large = [
         pltpu.make_async_copy(fields_hbm.at[rows[t]], fields_ref.at[rows[t]], in_sems.at[t])
-        for t in range(M)
+        for t in range(tiles)
     ]
     large[0].start()
     for copy in small:
         copy.start()
     for copy in large[1:]:
         copy.start()
+    for copy in small:
+        copy.wait()
+    bias = column(bias_ref[...])[:V]
     back = []
-    for t in range(M):
-        large[t].wait()
-        unit, _ = unit_of(fields_ref[rows[t]].astype(f32))
-        if t == 0:
-            for copy in small:
-                copy.wait()
-            bias = column(bias_ref[...])[:V]
-        normed = (unit * gain_ref[...]).astype(bf16)
-        normed_ref[rows[t]] = normed
-        back.append(pltpu.make_async_copy(normed_ref.at[rows[t]], normed_hbm.at[rows[t]], out_sems.at[t, 1]))
-        back[-1].start()
-        pred = lax.dot_general(weight_ref[...], normed, NT, preferred_element_type=f32)
-        pred_ref[t] = pred + bias
-        back.append(pltpu.make_async_copy(pred_ref.at[t], pred_hbm.at[t], out_sems.at[t, 0]))
-        back[-1].start()
+    for t in range(tiles + 1):
+        if t < tiles:
+            large[t].wait()
+            for start in range(t * TILE, (t + 1) * TILE, BLOCK):
+                block = slice(start, start + BLOCK)
+                normed_ref[block] = scaled_rows(fields_ref, block, gain_ref[...]).astype(bf16)
+            back.append(pltpu.make_async_copy(normed_ref.at[rows[t]], normed_hbm.at[rows[t]], out_sems.at[t, 1]))
+            back[-1].start()
+        if t > 0:
+            done = normed_ref[rows[t - 1]]
+            pred = lax.dot_general(weight_ref[...], done, NT, preferred_element_type=f32)
+            first = (t - 1) * slots
+            for k in range(slots):
+                pred_ref[first + k] = pred[:, k * LANES : (k + 1) * LANES] + bias
+            here = pl.ds(first, slots)
+            back.append(pltpu.make_async_copy(pred_ref.at[here], pred_hbm.at[here], out_sems.at[t - 1, 0]))
+            back[-1].start()
     for copy in back:
         copy.wait()
 
 
 def forward(fields, weight, bias, gain):
+    tiles = LOCAL // TILE
     return pl.pallas_call(
         forward_kernel,
         in_specs=[HBM] * 4,
-        out_specs=[HBM, HBM],
+        out_specs=[HBM] * 2,
         out_shape=[
             jax.ShapeDtypeStruct((M, V, LANES), f32),
             jax.ShapeDtypeStruct((LOCAL, D), bf16),
@@ -104,41 +120,43 @@
             pltpu.VMEM((1, D), f32),
             pltpu.VMEM((M, V, LANES), f32),
             pltpu.VMEM((LOCAL, D), bf16),
-            pltpu.SemaphoreType.DMA((M + 3,)),
-            pltpu.SemaphoreType.DMA((M, 2)),
+            pltpu.SemaphoreType.DMA((tiles + 3,)),
+            pltpu.SemaphoreType.DMA((tiles, 2)),
         ],
         compiler_params=params(FORWARD_VMEM),
-        cost_estimate=pl.CostEstimate(flops=2 * V * D * LOCAL, bytes_accessed=6 << 20, transcendentals=0),
+        cost_estimate=pl.CostEstimate(flops=2 * V * D * LOCAL, bytes_accessed=3 << 20, transcendentals=0),
     )(fields, weight, bias, gain)
 
 
-def residual_kernel(fields_ref, gain_ref, normed_ref, out_ref):
-    unit, _ = unit_of(fields_ref[...].astype(f32))
-    out_ref[...] = (unit * gain_ref[...] - normed_ref[...].astype(f32)).astype(bf16)
-
-
-def residual(fields, gain, normed):
+def residual_kernel(fields_ref, gain_ref, resid_ref):
+    for start in range(0, TILE, BLOCK):
+        block = slice(start, start + BLOCK)
+        scaled = scaled_rows(fields_ref, block, gain_ref[...])
+        rest = scaled - scaled.astype(bf16).astype(f32)
+        resid_ref[block] = (rest * RESIDUAL_SCALE).astype(f8)
+
+
+def residual(fields, gain):
     block = pl.BlockSpec((TILE, D), lambda i: (i, 0))
     return pl.pallas_call(
         residual_kernel,
         grid=(LOCAL // TILE,),
-        in_specs=[block, pl.BlockSpec((1, D), lambda i: (0, 0)), block],
+        in_specs=[block, pl.BlockSpec((1, D), lambda i: (0, 0))],
         out_specs=block,
-        out_shape=jax.ShapeDtypeStruct((LOCAL, D), bf16),
+        out_shape=jax.ShapeDtypeStruct((2 * LOCAL, D), f8),
         compiler_params=params(RESIDUAL_VMEM),
         cost_estimate=pl.CostEstimate(flops=12 * D * LOCAL, bytes_accessed=6 << 20, transcendentals=0),
-    )(fields, gain, normed)
+    )(fields, gain)
 
 
 def pair_kernel(slot_ref, pred_ref, obs_ref, lat_ref, vw_ref, grad_ref, loss_ref):
-    count = pred_ref.shape[1]
     here = pl.ds(pl.multiple_of(slot_ref[0] * LANES, LANES), LANES)
     vw = column(vw_ref[...])
     observed = obs_ref[:, here].astype(f32)
     lat = lat_ref[pl.ds(slot_ref[0], 1), :]
     loss = jnp.zeros((8, LANES), f32)
-    for start in range(0, count, 8):
-        rows = min(8, count - start)
+    for start in range(0, V, 8):
+        rows = min(8, V - start)
         part = slice(start, start + rows)
         obs = observed[part]
         pred = [pred_ref[m, part] for m in range(M)]
@@ -178,9 +196,9 @@
     return pl.pallas_call(
         pair_kernel,
         in_specs=[SMEM] + [VMEM] * 4,
-        out_specs=[pl.BlockSpec(pred.shape, lambda: (0, 0, 0)), VMEM],
+        out_specs=[VMEM] * 2,
         out_shape=[
-            jax.ShapeDtypeStruct(pred.shape, f32),
+            jax.ShapeDtypeStruct((M, V, LANES), f32),
             jax.ShapeDtypeStruct((8, LANES), f32),
         ],
         compiler_params=params(),
@@ -211,8 +229,8 @@
     for t in range(tiles):
         copies[t].wait()
         rows = slice(t * TILE, (t + 1) * TILE)
-        rest = rest + jnp.dot(grad[:, rows], resid_ref[rows], preferred_element_type=f32)
-    part_gain = weight_ref[...].astype(f32) * (out_ref[:V] + rest)
+        rest = rest + jnp.dot(grad[:, rows], resid_ref[rows].astype(bf16), preferred_element_type=f32)
+    part_gain = weight_ref[...].astype(f32) * (out_ref[:V] + rest * (1.0 / RESIDUAL_SCALE))
     part_gain = jnp.sum(part_gain, axis=0, keepdims=True) / gain_ref[...]
     out_ref[V:] = jnp.concatenate([part_gain, misc, lat, jnp.zeros((1, D), f32)], axis=0)
 
@@ -224,7 +242,7 @@
         out_specs=VMEM,
         out_shape=jax.ShapeDtypeStruct((ROWS, D), f32),
         scratch_shapes=[
-            pltpu.VMEM((LOCAL, D), bf16),
+            pltpu.VMEM((LOCAL, D), f8),
             pltpu.SemaphoreType.DMA((LOCAL // TILE,)),
         ],
         compiler_params=params(WEIGHT_VMEM),
@@ -340,14 +358,14 @@
     gain_row = gain.reshape(1, D)
     vw_row = var_weight.reshape(1, V)
     lat = lat_weight.reshape(M, LANES)
-    slot = lax.axis_index(MEMBER).astype(jnp.int32).reshape(1)
+    slot = lax.axis_index(PLACE).astype(jnp.int32).reshape(1)
     core = lax.axis_index("core").astype(jnp.int32).reshape(1)
     pred, normed = forward(fields, weight, bias.reshape(1, V), gain_row)
-    pred = swap(pred, MEMBER)
-    resid = residual(fields, gain_row, normed)
+    pred = swap(pred, PLACE)
+    resid = residual(fields, gain_row)
     pred, resid = lax.optimization_barrier((pred, resid))
     grad, loss = pair(slot, pred, observed, lat, vw_row)
-    grad = swap(grad, MEMBER)
+    grad = swap(grad, PLACE)
     sums = weight_part(grad, weight, gain_row, lat, loss, normed, resid)
     sums = lax.all_gather(sums, "core")
     sums = fold(core, sums)

time: 115 us -> 112 us (0.974)
  Pallas kernels: 19.4 us -> 16.9 us
    all_gather x1, blocking collectives: 5.21 us -> 2.55 us  [shards(): sums = lax.all_gather(sums, 'core')]
    pallas_call x2, Pallas kernels: 6.35 us -> 4.54 us  [the longest x1 3.95 us: forward(): pl.pallas_call(forward_kernel, in_specs=[HBM] * 4, out_specs=[HBM] * 2, o...]
    all_to_all x2, blocking collectives: 47.2 us -> 48.8 us  [swap(): return lax.all_to_all(array, axes, split_axis=0, concat_axis=0, tiled=True)]
where the time goes in v5:
time: 112 us
  blocking collectives  56.7 us (51%)
  starting transfers between devices  20.3 us (18%)
  waiting for transfers between devices  17.3 us (15%)
  Pallas kernels  16.9 us (15%)
    all_to_all x2, blocking collectives, swap(): return lax.all_to_all(array, axes, split_axis=0, concat_axis=0, tiled=True)  48.8 us
    all_to_all x2, starting transfers between devices, swap(): return lax.all_to_all(array, axes, split_axis=0, concat_axis=0, tiled=True)  20.3 us
    all_to_all x2, waiting for transfers between devices, swap(): return lax.all_to_all(array, axes, split_axis=0, concat_axis=0, tiled=True)  17.3 us
    all_gather x1, blocking collectives, shards(): sums = lax.all_gather(sums.reshape(D // 2, LANES), 'core', tiled=True)  5.39 us
    pallas_call x1, Pallas kernels, residual(): pl.pallas_call(residual_kernel, grid=(LOCAL // TILE,), in_specs=[block, p...  4.66 us
    pallas_call x1, Pallas kernels, forward(): pl.pallas_call(forward_kernel, in_specs=[HBM] * 4, out_specs=[HBM] * 2, o...  3.95 us
    pallas_call x1, Pallas kernels, fields_part(): pl.pallas_call(functools.partial(fields_kernel, points_total), grid=(LOCA...  3.76 us
    all_gather x1, blocking collectives, shards(): sums = lax.all_gather(sums, 'core')  2.55 us
  transfers between devices with their start and end apart: 2, of which 2 were waited for; matrix products, arithmetic and copies ran while one was open for 0% of the time, Pallas kernels for 8%

profile of v5, /device:TPU:1, one launch (start us, length us, event | category | flops | bytes accessed | tf_op | source)
XLA Modules:
  0.0 111.9 jit_solution(7523059919921063431)
XLA Ops:
  0.6 3.9 %shard_map.110 = (f32[8,100,128]{2,1,0:T(8,128)}, bf16[1024,1024]{1,0:T(8,128)(2,1)}) custom-call(bf16[1024,1024]{1,0:T(8,128)(2,1)} %bitcast.16, bf16[100,1024]{1,0:T(8,128)(2,1)} %weight_ref.3, f32[1,100]{1,0:T(1,128)} %bitcast.31, f32[1,1024]{1,0:T(1,128)} %bitcast.22), custom_call_target="tpu_custom_call" | custom-call | flops 209715200 | bytes 3145728 | tf_op jit(solution)/shard_map/pallas_call | solution.py:108
  4.6 10.3 %all-to-all-start = ((f32[8,100,128]{2,1,0:T(8,128)}), f32[8,100,128]{2,1,0:T(8,128)S(1)}, u32[]{:S(2)}, u32[]{:S(2)}) async-start(f32[8,100,128]{2,1,0:T(8,128)} %get-tuple-element.17), calls=%async_computation | async-start | bytes 851968 | tf_op jit(solution)/shard_map/all_to_all | solution.py:353
  14.9 0.0 copy-start.3
  14.9 0.0 copy-start.5
  14.9 0.0 copy-start.6
  14.9 0.0 copy-start.1
  14.9 0.0 copy-start.2
  14.9 0.0 copy-start.4
  14.9 4.7 %shard_map.111.resid_hbm = f8e4m3fn[2048,1024]{1,0:T(32,128)(4,1)} custom-call(bf16[1024,1024]{1,0:T(8,128)(2,1)} %bitcast.17, f32[1,1024]{1,0:T(1,128)} %bitcast.23), custom_call_target="tpu_custom_call" | custom-call | flops 12582912 | bytes 6291456 | tf_op jit(solution)/shard_map/pallas_call | solution.py:141
  19.6 8.7 %all-to-all-done.pred_ref = f32[8,100,128]{2,1,0:T(8,128)S(1)} async-done(((f32[8,100,128]{2,1,0:T(8,128)}), f32[8,100,128]{2,1,0:T(8,128)S(1)}, u32[]{:S(2)}, u32[]{:S(2)}) %all-to-all-start) | async-done | bytes 409632 | tf_op jit(solution)/shard_map/all_to_all | solution.py:353
  28.2 0.0 copy-done.3
  28.2 0.0 copy-done.5
  28.2 0.0 copy-done.6
  28.2 0.6 shard_map.112
  28.8 16.6 %all_to_all.20.grad_ref = f32[8,100,128]{2,1,0:T(8,128)S(1)} all-to-all(f32[8,100,128]{2,1,0:T(8,128)S(1)} %get-tuple-element.19), channel_id=1, replica_groups=mesh['x'=4,'y_lo'=2,'z'=8,'y_hi'=4,'core'=2] {'core','y_hi'}, dimensions={0} | all-to-all | bytes 819200 | tf_op jit(solution)/shard_map/all_to_all | solution.py:353
  45.5 0.0 copy-done.1
  45.5 0.0 copy-done.2
  45.5 0.0 copy-done.4
  45.5 1.9 %shard_map.113 = f32[104,1024]{1,0:T(8,128)S(1)} custom-call(f32[8,100,128]{2,1,0:T(8,128)S(1)} %all_to_all.20.grad_ref, bf16[100,1024]{1,0:T(8,128)(2,1)S(1)} %copy-done.2, f32[1,1024]{1,0:T(1,128)S(1)} %bitcast.24, f32[8,128]{1,0:T(8,128)S(1)} %bitcast.27, f32[8,128]{1,0:T(8,128)S(1)} %get-tuple-element.20.loss_ref, bf16[1024,1024]{1,0:T(8,128)(2,1)S(1)} %copy-done.1, ...), custom_call_target="tpu_custom_call" | custom-call | flops 419430400 | bytes 4194304 | tf_op jit(solution)/shard_map/pallas_call | solution.py:239
  47.4 0.0 copy-start
  47.4 2.5 %all-gather = f32[208,1024]{1,0:T(8,128)S(1)} all-gather(f32[104,1024]{1,0:T(8,128)S(1)} %shard_map.113), channel_id=2, replica_groups=mesh['x'=4,'y_lo'=2,'z'=8,'y_hi'=4,'core'=2] {'core'}, dimensions={0}, use_global_device_ids=true | all-gather | bytes 1277952 | tf_op jit(solution)/shard_map/all_gather | solution.py:370
  50.0 0.1 shard_map.114
  50.1 32.1 %all_to_all.21 = f32[256,2,128]{2,1,0:T(2,128)S(1)} all-to-all(f32[256,2,128]{2,1,0:T(2,128)S(1)} %bitcast.21), channel_id=1, replica_groups=mesh['x'=4,'y_lo'=2,'z'=8,'y_hi'=4,'core'=2] {'x','y_hi','y_lo','z'}, dimensions={0} | all-to-all | bytes 524288 | tf_op jit(solution)/shard_map/all_to_all | solution.py:353
  82.2 0.8 shard_map.115
  83.0 10.0 %all-to-all-start.3 = ((f32[256,2,128]{2,1,0:T(2,128)}), f32[256,2,128]{2,1,0:T(2,128)S(1)}, u32[]{:S(2)}, u32[]{:S(2)}) async-start(f32[256,2,128]{2,1,0:T(2,128)} %bitcast.11), calls=%async_computation.3 | async-start | bytes 524288 | tf_op jit(solution)/shard_map/all_to_all | solution.py:353
  93.0 0.0 copy-done
  93.0 3.8 %shard_map.116 = bf16[1024,1024]{1,0:T(8,128)(2,1)} custom-call(bf16[1024,1024]{1,0:T(8,128)(2,1)S(1)} %bitcast.18, f32[8,100,128]{2,1,0:T(8,128)S(1)} %all_to_all.20.grad_ref, bf16[100,1024]{1,0:T(8,128)(2,1)S(1)} %copy-done.2, f32[1,1024]{1,0:T(1,128)S(1)} %bitcast.25, f32[8,128]{1,0:T(8,128)S(1)} %get-tuple-element.23.lat_ref), custom_call_target="tpu_custom_call" | custom-call | flops 209715200 | bytes 12582912 | tf_op jit(solution)/shard_map/pallas_call | solution.py:335
  96.8 8.6 %all-to-all-done.3 = f32[256,2,128]{2,1,0:T(2,128)S(1)} async-done(((f32[256,2,128]{2,1,0:T(2,128)}), f32[256,2,128]{2,1,0:T(2,128)S(1)}, u32[]{:S(2)}, u32[]{:S(2)}) %all-to-all-start.3) | async-done | bytes 262176 | tf_op jit(solution)/shard_map/all_to_all | solution.py:353
  105.4 5.4 %all_gather.11.parts_ref = f32[1024,128]{1,0:T(8,128)S(1)} all-gather(f32[512,128]{1,0:T(8,128)S(1)} %bitcast.30), channel_id=1, replica_groups=mesh['x'=4,'y_lo'=2,'z'=8,'y_hi'=4,'core'=2] {'core'}, dimensions={0}, use_global_device_ids=true | all-gather | bytes 786432 | tf_op jit(solution)/shard_map/all_gather | solution.py:376
  110.8 1.1 shard_map.117
Async XLA Ops:
  4.6 23.7 %all-to-all-start = ((f32[8,100,128]{2,1,0:T(8,128)}), f32[8,100,128]{2,1,0:T(8,128)S(1)}, u32[]{:S(2)}, u32[]{:S(2)}) async-start(f32[8,100,128]{2,1,0:T(8,128)} %get-tuple-element.17), calls=%async_computation | async-start | bytes 851968 | tf_op jit(solution)/shard_map/all_to_all | solution.py:353
  14.9 13.4 %copy-start.3 = (bf16[100,1024]{1,0:T(8,128)(2,1)S(1)}, bf16[100,1024]{1,0:T(8,128)(2,1)}, u32[]{:S(2)}) copy-start(bf16[100,1024]{1,0:T(8,128)(2,1)} %obs_ref.1) | copy-start | bytes 614404
  14.9 13.4 %copy-start.5 = (f32[1024]{0:T(1024)S(1)}, f32[1024]{0:T(1024)}, u32[]{:S(2)}) copy-start(f32[1024]{0:T(1024)} %param.9) | copy-start | bytes 12292
  14.9 13.4 %copy-start.6 = (f32[100]{0:T(128)S(1)}, f32[100]{0:T(128)}, u32[]{:S(2)}) copy-start(f32[100]{0:T(128)} %param.10) | copy-start | bytes 1204
  14.9 30.6 %copy-start.1 = (bf16[1024,1024]{1,0:T(8,128)(2,1)S(1)}, bf16[1024,1024]{1,0:T(8,128)(2,1)}, u32[]{:S(2)}) copy-start(bf16[1024,1024]{1,0:T(8,128)(2,1)} %get-tuple-element.21.normed_ref) | copy-start | bytes 6291460
  14.9 30.6 %copy-start.2 = (bf16[100,1024]{1,0:T(8,128)(2,1)S(1)}, bf16[100,1024]{1,0:T(8,128)(2,1)}, u32[]{:S(2)}) copy-start(bf16[100,1024]{1,0:T(8,128)(2,1)} %weight_ref.3) | copy-start | bytes 614404
  14.9 30.6 %copy-start.4 = (f32[1024]{0:T(1024)S(1)}, f32[1024]{0:T(1024)}, u32[]{:S(2)}) copy-start(f32[1024]{0:T(1024)} %param.13) | copy-start | bytes 12292
  47.4 45.6 %copy-start = (bf16[1,1024,1024]{2,1,0:T(8,128)(2,1)S(1)}, bf16[1,1024,1024]{2,1,0:T(8,128)(2,1)}, u32[]{:S(2)}) copy-start(bf16[1,1024,1024]{2,1,0:T(8,128)(2,1)} %param.7) | copy-start | bytes 6291460
  83.0 22.4 %all-to-all-start.3 = ((f32[256,2,128]{2,1,0:T(2,128)}), f32[256,2,128]{2,1,0:T(2,128)S(1)}, u32[]{:S(2)}, u32[]{:S(2)}) async-start(f32[256,2,128]{2,1,0:T(2,128)} %bitcast.11), calls=%async_computation.3 | async-start | bytes 524288 | tf_op jit(solution)/shard_map/all_to_all | solution.py:353

commit v6 on v5

--- a/solution.py
+++ b/solution.py
@@ -17,6 +17,7 @@
 LANES = 128
 TILE = 256
 BLOCK = 32
+STEP = 512
 ROWS = 104
 GAIN_ROW, MISC_ROW, LAT_ROW = 100, 101, 102
 GRID = ("x", "y_lo", "z")
@@ -71,25 +72,37 @@
     ]
     large = [
         pltpu.make_async_copy(fields_hbm.at[rows[t]], fields_ref.at[rows[t]], in_sems.at[t])
-        for t in range(tiles)
+        for t in range(1, tiles)
     ]
-    large[0].start()
+    halves = [
+        pltpu.make_async_copy(fields_hbm.at[half], fields_ref.at[half], sem)
+        for half, sem in (
+            (pl.ds(0, TILE // 2), in_sems.at[0]),
+            (pl.ds(TILE // 2, TILE // 2), in_sems.at[tiles + 3]),
+        )
+    ]
+    halves[0].start()
     for copy in small:
         copy.start()
-    for copy in large[1:]:
+    for copy in halves[1:] + large:
         copy.start()
-    for copy in small:
-        copy.wait()
-    bias = column(bias_ref[...])[:V]
+    small[0].wait()
     back = []
     for t in range(tiles + 1):
         if t < tiles:
-            large[t].wait()
+            if t > 0:
+                large[t - 1].wait()
             for start in range(t * TILE, (t + 1) * TILE, BLOCK):
+                if t == 0 and start % (TILE // 2) == 0:
+                    halves[start // (TILE // 2)].wait()
                 block = slice(start, start + BLOCK)
                 normed_ref[block] = scaled_rows(fields_ref, block, gain_ref[...]).astype(bf16)
             back.append(pltpu.make_async_copy(normed_ref.at[rows[t]], normed_hbm.at[rows[t]], out_sems.at[t, 1]))
             back[-1].start()
+        if t == 1:
+            for copy in small[1:]:
+                copy.wait()
+            bias = column(bias_ref[...])[:V]
         if t > 0:
             done = normed_ref[rows[t - 1]]
             pred = lax.dot_general(weight_ref[...], done, NT, preferred_element_type=f32)
@@ -120,7 +133,7 @@
             pltpu.VMEM((1, D), f32),
             pltpu.VMEM((M, V, LANES), f32),
             pltpu.VMEM((LOCAL, D), bf16),
-            pltpu.SemaphoreType.DMA((tiles + 3,)),
+            pltpu.SemaphoreType.DMA((tiles + 4,)),
             pltpu.SemaphoreType.DMA((tiles, 2)),
         ],
         compiler_params=params(FORWARD_VMEM),
@@ -207,10 +220,10 @@
 
 
 def weight_kernel(grad_ref, weight_ref, gain_ref, lat_ref, loss_ref, normed_ref, resid_hbm, out_ref, resid_ref, sems):
-    tiles = LOCAL // TILE
+    tiles = LOCAL // STEP
     copies = [
         pltpu.make_async_copy(
-            resid_hbm.at[pl.ds(t * TILE, TILE)], resid_ref.at[pl.ds(t * TILE, TILE)], sems.at[t]
+            resid_hbm.at[pl.ds(t * STEP, STEP)], resid_ref.at[pl.ds(t * STEP, STEP)], sems.at[t]
         )
         for t in range(tiles)
     ]
@@ -228,7 +241,7 @@
     rest = jnp.zeros((V, D), f32)
     for t in range(tiles):
         copies[t].wait()
-        rows = slice(t * TILE, (t + 1) * TILE)
+        rows = slice(t * STEP, (t + 1) * STEP)
         rest = rest + jnp.dot(grad[:, rows], resid_ref[rows].astype(bf16), preferred_element_type=f32)
     part_gain = weight_ref[...].astype(f32) * (out_ref[:V] + rest * (1.0 / RESIDUAL_SCALE))
     part_gain = jnp.sum(part_gain, axis=0, keepdims=True) / gain_ref[...]
@@ -243,7 +256,7 @@
         out_shape=jax.ShapeDtypeStruct((ROWS, D), f32),
         scratch_shapes=[
             pltpu.VMEM((LOCAL, D), f8),
-            pltpu.SemaphoreType.DMA((LOCAL // TILE,)),
+            pltpu.SemaphoreType.DMA((LOCAL // STEP,)),
         ],
         compiler_params=params(WEIGHT_VMEM),
         cost_estimate=pl.CostEstimate(flops=4 * V * D * LOCAL, bytes_accessed=4 << 20, transcendentals=0),

time: 112 us -> 112 us (level)
  no operation moved by 1% of the time
where the time goes in v6:
time: 112 us
  blocking collectives  56.7 us (51%)
  starting transfers between devices  20.3 us (18%)
  waiting for transfers between devices  17.3 us (15%)
  Pallas kernels  17 us (15%)
    all_to_all x2, blocking collectives, swap(): return lax.all_to_all(array, axes, split_axis=0, concat_axis=0, tiled=True)  48.7 us
    all_to_all x2, starting transfers between devices, swap(): return lax.all_to_all(array, axes, split_axis=0, concat_axis=0, tiled=True)  20.3 us
    all_to_all x2, waiting for transfers between devices, swap(): return lax.all_to_all(array, axes, split_axis=0, concat_axis=0, tiled=True)  17.3 us
    all_gather x1, blocking collectives, shards(): sums = lax.all_gather(sums.reshape(D // 2, LANES), 'core', tiled=True)  5.39 us
    pallas_call x1, Pallas kernels, residual(): pl.pallas_call(residual_kernel, grid=(LOCAL // TILE,), in_specs=[block, p...  4.66 us
    pallas_call x1, Pallas kernels, forward(): pl.pallas_call(forward_kernel, in_specs=[HBM] * 4, out_specs=[HBM] * 2, o...  4.18 us
    pallas_call x1, Pallas kernels, fields_part(): pl.pallas_call(functools.partial(fields_kernel, points_total), grid=(LOCA...  3.76 us
    all_gather x1, blocking collectives, shards(): sums = lax.all_gather(sums, 'core')  2.55 us
  transfers between devices with their start and end apart: 2, of which 2 were waited for; matrix products, arithmetic and copies ran while one was open for 0% of the time, Pallas kernels for 8%

profile of v6, /device:TPU:1, one launch (start us, length us, event | category | flops | bytes accessed | tf_op | source)
XLA Modules:
  0.0 112.0 jit_solution(7100615018108419298)
XLA Ops:
  0.6 4.2 %shard_map.110 = (f32[8,100,128]{2,1,0:T(8,128)}, bf16[1024,1024]{1,0:T(8,128)(2,1)}) custom-call(bf16[1024,1024]{1,0:T(8,128)(2,1)} %bitcast.16, bf16[100,1024]{1,0:T(8,128)(2,1)} %weight_ref.3, f32[1,100]{1,0:T(1,128)} %bitcast.31, f32[1,1024]{1,0:T(1,128)} %bitcast.22), custom_call_target="tpu_custom_call" | custom-call | flops 209715200 | bytes 3145728 | tf_op jit(solution)/shard_map/pallas_call | solution.py:121
  4.8 10.3 %all-to-all-start = ((f32[8,100,128]{2,1,0:T(8,128)}), f32[8,100,128]{2,1,0:T(8,128)S(1)}, u32[]{:S(2)}, u32[]{:S(2)}) async-start(f32[8,100,128]{2,1,0:T(8,128)} %get-tuple-element.17), calls=%async_computation | async-start | bytes 851968 | tf_op jit(solution)/shard_map/all_to_all | solution.py:366
  15.1 0.0 copy-start.3
  15.1 0.0 copy-start.5
  15.1 0.0 copy-start.6
  15.1 0.0 copy-start.1
  15.1 0.0 copy-start.2
  15.1 0.0 copy-start.4
  15.1 4.7 %shard_map.111.resid_hbm = f8e4m3fn[2048,1024]{1,0:T(32,128)(4,1)} custom-call(bf16[1024,1024]{1,0:T(8,128)(2,1)} %bitcast.17, f32[1,1024]{1,0:T(1,128)} %bitcast.23), custom_call_target="tpu_custom_call" | custom-call | flops 12582912 | bytes 6291456 | tf_op jit(solution)/shard_map/pallas_call | solution.py:154
  19.8 8.7 %all-to-all-done.pred_ref = f32[8,100,128]{2,1,0:T(8,128)S(1)} async-done(((f32[8,100,128]{2,1,0:T(8,128)}), f32[8,100,128]{2,1,0:T(8,128)S(1)}, u32[]{:S(2)}, u32[]{:S(2)}) %all-to-all-start) | async-done | bytes 409632 | tf_op jit(solution)/shard_map/all_to_all | solution.py:366
  28.5 0.0 copy-done.3
  28.5 0.0 copy-done.5
  28.5 0.0 copy-done.6
  28.5 0.6 shard_map.112
  29.1 16.6 %all_to_all.20.grad_ref = f32[8,100,128]{2,1,0:T(8,128)S(1)} all-to-all(f32[8,100,128]{2,1,0:T(8,128)S(1)} %get-tuple-element.19), channel_id=1, replica_groups=mesh['x'=4,'y_lo'=2,'z'=8,'y_hi'=4,'core'=2] {'core','y_hi'}, dimensions={0} | all-to-all | bytes 819200 | tf_op jit(solution)/shard_map/all_to_all | solution.py:366
  45.7 0.0 copy-done.1
  45.7 0.0 copy-done.2
  45.7 0.0 copy-done.4
  45.7 1.8 %shard_map.113 = f32[104,1024]{1,0:T(8,128)S(1)} custom-call(f32[8,100,128]{2,1,0:T(8,128)S(1)} %all_to_all.20.grad_ref, bf16[100,1024]{1,0:T(8,128)(2,1)S(1)} %copy-done.2, f32[1,1024]{1,0:T(1,128)S(1)} %bitcast.24, f32[8,128]{1,0:T(8,128)S(1)} %bitcast.27, f32[8,128]{1,0:T(8,128)S(1)} %get-tuple-element.20.loss_ref, bf16[1024,1024]{1,0:T(8,128)(2,1)S(1)} %copy-done.1, ...), custom_call_target="tpu_custom_call" | custom-call | flops 419430400 | bytes 4194304 | tf_op jit(solution)/shard_map/pallas_call | solution.py:252
  47.5 0.0 copy-start
  47.5 2.5 %all-gather = f32[208,1024]{1,0:T(8,128)S(1)} all-gather(f32[104,1024]{1,0:T(8,128)S(1)} %shard_map.113), channel_id=2, replica_groups=mesh['x'=4,'y_lo'=2,'z'=8,'y_hi'=4,'core'=2] {'core'}, dimensions={0}, use_global_device_ids=true | all-gather | bytes 1277952 | tf_op jit(solution)/shard_map/all_gather | solution.py:383
  50.1 0.1 shard_map.114
  50.2 32.1 %all_to_all.21 = f32[256,2,128]{2,1,0:T(2,128)S(1)} all-to-all(f32[256,2,128]{2,1,0:T(2,128)S(1)} %bitcast.21), channel_id=1, replica_groups=mesh['x'=4,'y_lo'=2,'z'=8,'y_hi'=4,'core'=2] {'x','y_hi','y_lo','z'}, dimensions={0} | all-to-all | bytes 524288 | tf_op jit(solution)/shard_map/all_to_all | solution.py:366
  82.3 0.8 shard_map.115
  83.1 10.0 %all-to-all-start.3 = ((f32[256,2,128]{2,1,0:T(2,128)}), f32[256,2,128]{2,1,0:T(2,128)S(1)}, u32[]{:S(2)}, u32[]{:S(2)}) async-start(f32[256,2,128]{2,1,0:T(2,128)} %bitcast.11), calls=%async_computation.3 | async-start | bytes 524288 | tf_op jit(solution)/shard_map/all_to_all | solution.py:366
  93.1 0.0 copy-done
  93.1 3.8 %shard_map.116 = bf16[1024,1024]{1,0:T(8,128)(2,1)} custom-call(bf16[1024,1024]{1,0:T(8,128)(2,1)S(1)} %bitcast.18, f32[8,100,128]{2,1,0:T(8,128)S(1)} %all_to_all.20.grad_ref, bf16[100,1024]{1,0:T(8,128)(2,1)S(1)} %copy-done.2, f32[1,1024]{1,0:T(1,128)S(1)} %bitcast.25, f32[8,128]{1,0:T(8,128)S(1)} %get-tuple-element.23.lat_ref), custom_call_target="tpu_custom_call" | custom-call | flops 209715200 | bytes 12582912 | tf_op jit(solution)/shard_map/pallas_call | solution.py:348
  96.9 8.6 %all-to-all-done.3 = f32[256,2,128]{2,1,0:T(2,128)S(1)} async-done(((f32[256,2,128]{2,1,0:T(2,128)}), f32[256,2,128]{2,1,0:T(2,128)S(1)}, u32[]{:S(2)}, u32[]{:S(2)}) %all-to-all-start.3) | async-done | bytes 262176 | tf_op jit(solution)/shard_map/all_to_all | solution.py:366
  105.5 5.4 %all_gather.11.parts_ref = f32[1024,128]{1,0:T(8,128)S(1)} all-gather(f32[512,128]{1,0:T(8,128)S(1)} %bitcast.30), channel_id=1, replica_groups=mesh['x'=4,'y_lo'=2,'z'=8,'y_hi'=4,'core'=2] {'core'}, dimensions={0}, use_global_device_ids=true | all-gather | bytes 786432 | tf_op jit(solution)/shard_map/all_gather | solution.py:389
  110.9 1.1 shard_map.117
Async XLA Ops:
  4.8 23.7 %all-to-all-start = ((f32[8,100,128]{2,1,0:T(8,128)}), f32[8,100,128]{2,1,0:T(8,128)S(1)}, u32[]{:S(2)}, u32[]{:S(2)}) async-start(f32[8,100,128]{2,1,0:T(8,128)} %get-tuple-element.17), calls=%async_computation | async-start | bytes 851968 | tf_op jit(solution)/shard_map/all_to_all | solution.py:366
  15.1 13.4 %copy-start.3 = (bf16[100,1024]{1,0:T(8,128)(2,1)S(1)}, bf16[100,1024]{1,0:T(8,128)(2,1)}, u32[]{:S(2)}) copy-start(bf16[100,1024]{1,0:T(8,128)(2,1)} %obs_ref.1) | copy-start | bytes 614404
  15.1 13.4 %copy-start.5 = (f32[1024]{0:T(1024)S(1)}, f32[1024]{0:T(1024)}, u32[]{:S(2)}) copy-start(f32[1024]{0:T(1024)} %param.9) | copy-start | bytes 12292
  15.1 13.4 %copy-start.6 = (f32[100]{0:T(128)S(1)}, f32[100]{0:T(128)}, u32[]{:S(2)}) copy-start(f32[100]{0:T(128)} %param.10) | copy-start | bytes 1204
  15.1 30.6 %copy-start.1 = (bf16[1024,1024]{1,0:T(8,128)(2,1)S(1)}, bf16[1024,1024]{1,0:T(8,128)(2,1)}, u32[]{:S(2)}) copy-start(bf16[1024,1024]{1,0:T(8,128)(2,1)} %get-tuple-element.21.normed_ref) | copy-start | bytes 6291460
  15.1 30.6 %copy-start.2 = (bf16[100,1024]{1,0:T(8,128)(2,1)S(1)}, bf16[100,1024]{1,0:T(8,128)(2,1)}, u32[]{:S(2)}) copy-start(bf16[100,1024]{1,0:T(8,128)(2,1)} %weight_ref.3) | copy-start | bytes 614404
  15.1 30.6 %copy-start.4 = (f32[1024]{0:T(1024)S(1)}, f32[1024]{0:T(1024)}, u32[]{:S(2)}) copy-start(f32[1024]{0:T(1024)} %param.13) | copy-start | bytes 12292
  47.5 45.6 %copy-start = (bf16[1,1024,1024]{2,1,0:T(8,128)(2,1)S(1)}, bf16[1,1024,1024]{2,1,0:T(8,128)(2,1)}, u32[]{:S(2)}) copy-start(bf16[1,1024,1024]{2,1,0:T(8,128)(2,1)} %param.7) | copy-start | bytes 6291460
  83.1 22.4 %all-to-all-start.3 = ((f32[256,2,128]{2,1,0:T(2,128)}), f32[256,2,128]{2,1,0:T(2,128)S(1)}, u32[]{:S(2)}, u32[]{:S(2)}) async-start(f32[256,2,128]{2,1,0:T(2,128)} %bitcast.11), calls=%async_computation.3 | async-start | bytes 524288 | tf_op jit(solution)/shard_map/all_to_all | solution.py:366

commit v7 on v5

--- a/solution.py
+++ b/solution.py
@@ -17,6 +17,7 @@
 LANES = 128
 TILE = 256
 BLOCK = 32
+STEP = 512
 ROWS = 104
 GAIN_ROW, MISC_ROW, LAT_ROW = 100, 101, 102
 GRID = ("x", "y_lo", "z")
@@ -207,10 +208,10 @@
 
 
 def weight_kernel(grad_ref, weight_ref, gain_ref, lat_ref, loss_ref, normed_ref, resid_hbm, out_ref, resid_ref, sems):
-    tiles = LOCAL // TILE
+    tiles = LOCAL // STEP
     copies = [
         pltpu.make_async_copy(
-            resid_hbm.at[pl.ds(t * TILE, TILE)], resid_ref.at[pl.ds(t * TILE, TILE)], sems.at[t]
+            resid_hbm.at[pl.ds(t * STEP, STEP)], resid_ref.at[pl.ds(t * STEP, STEP)], sems.at[t]
         )
         for t in range(tiles)
     ]
@@ -228,7 +229,7 @@
     rest = jnp.zeros((V, D), f32)
     for t in range(tiles):
         copies[t].wait()
-        rows = slice(t * TILE, (t + 1) * TILE)
+        rows = slice(t * STEP, (t + 1) * STEP)
         rest = rest + jnp.dot(grad[:, rows], resid_ref[rows].astype(bf16), preferred_element_type=f32)
     part_gain = weight_ref[...].astype(f32) * (out_ref[:V] + rest * (1.0 / RESIDUAL_SCALE))
     part_gain = jnp.sum(part_gain, axis=0, keepdims=True) / gain_ref[...]
@@ -243,7 +244,7 @@
         out_shape=jax.ShapeDtypeStruct((ROWS, D), f32),
         scratch_shapes=[
             pltpu.VMEM((LOCAL, D), f8),
-            pltpu.SemaphoreType.DMA((LOCAL // TILE,)),
+            pltpu.SemaphoreType.DMA((LOCAL // STEP,)),
         ],
         compiler_params=params(WEIGHT_VMEM),
         cost_estimate=pl.CostEstimate(flops=4 * V * D * LOCAL, bytes_accessed=4 << 20, transcendentals=0),

time: 112 us -> 112 us (level)
  no operation moved by 1% of the time
where the time goes in v7:
time: 112 us
  blocking collectives  56.7 us (51%)
  starting transfers between devices  20.3 us (18%)
  waiting for transfers between devices  17.3 us (15%)
  Pallas kernels  16.8 us (15%)
    all_to_all x2, blocking collectives, swap(): return lax.all_to_all(array, axes, split_axis=0, concat_axis=0, tiled=True)  48.8 us
    all_to_all x2, starting transfers between devices, swap(): return lax.all_to_all(array, axes, split_axis=0, concat_axis=0, tiled=True)  20.3 us
    all_to_all x2, waiting for transfers between devices, swap(): return lax.all_to_all(array, axes, split_axis=0, concat_axis=0, tiled=True)  17.3 us
    all_gather x1, blocking collectives, shards(): sums = lax.all_gather(sums.reshape(D // 2, LANES), 'core', tiled=True)  5.39 us
    pallas_call x1, Pallas kernels, residual(): pl.pallas_call(residual_kernel, grid=(LOCAL // TILE,), in_specs=[block, p...  4.66 us
    pallas_call x1, Pallas kernels, forward(): pl.pallas_call(forward_kernel, in_specs=[HBM] * 4, out_specs=[HBM] * 2, o...  3.95 us
    pallas_call x1, Pallas kernels, fields_part(): pl.pallas_call(functools.partial(fields_kernel, points_total), grid=(LOCA...  3.76 us
    all_gather x1, blocking collectives, shards(): sums = lax.all_gather(sums, 'core')  2.55 us
  transfers between devices with their start and end apart: 2, of which 2 were waited for; matrix products, arithmetic and copies ran while one was open for 0% of the time, Pallas kernels for 8%

profile of v7, /device:TPU:1, one launch (start us, length us, event | category | flops | bytes accessed | tf_op | source)
XLA Modules:
  0.0 111.8 jit_solution(4508804658623477555)
XLA Ops:
  0.6 3.9 %shard_map.110 = (f32[8,100,128]{2,1,0:T(8,128)}, bf16[1024,1024]{1,0:T(8,128)(2,1)}) custom-call(bf16[1024,1024]{1,0:T(8,128)(2,1)} %bitcast.16, bf16[100,1024]{1,0:T(8,128)(2,1)} %weight_ref.3, f32[1,100]{1,0:T(1,128)} %bitcast.31, f32[1,1024]{1,0:T(1,128)} %bitcast.22), custom_call_target="tpu_custom_call" | custom-call | flops 209715200 | bytes 3145728 | tf_op jit(solution)/shard_map/pallas_call | solution.py:109
  4.6 10.3 %all-to-all-start = ((f32[8,100,128]{2,1,0:T(8,128)}), f32[8,100,128]{2,1,0:T(8,128)S(1)}, u32[]{:S(2)}, u32[]{:S(2)}) async-start(f32[8,100,128]{2,1,0:T(8,128)} %get-tuple-element.17), calls=%async_computation | async-start | bytes 851968 | tf_op jit(solution)/shard_map/all_to_all | solution.py:354
  14.9 0.0 copy-start.3
  14.9 0.0 copy-start.5
  14.9 0.0 copy-start.6
  14.9 0.0 copy-start.1
  14.9 0.0 copy-start.2
  14.9 0.0 copy-start.4
  14.9 4.7 %shard_map.111.resid_hbm = f8e4m3fn[2048,1024]{1,0:T(32,128)(4,1)} custom-call(bf16[1024,1024]{1,0:T(8,128)(2,1)} %bitcast.17, f32[1,1024]{1,0:T(1,128)} %bitcast.23), custom_call_target="tpu_custom_call" | custom-call | flops 12582912 | bytes 6291456 | tf_op jit(solution)/shard_map/pallas_call | solution.py:142
  19.6 8.7 %all-to-all-done.pred_ref = f32[8,100,128]{2,1,0:T(8,128)S(1)} async-done(((f32[8,100,128]{2,1,0:T(8,128)}), f32[8,100,128]{2,1,0:T(8,128)S(1)}, u32[]{:S(2)}, u32[]{:S(2)}) %all-to-all-start) | async-done | bytes 409632 | tf_op jit(solution)/shard_map/all_to_all | solution.py:354
  28.2 0.0 copy-done.3
  28.2 0.0 copy-done.5
  28.2 0.0 copy-done.6
  28.2 0.6 shard_map.112
  28.8 16.6 %all_to_all.20.grad_ref = f32[8,100,128]{2,1,0:T(8,128)S(1)} all-to-all(f32[8,100,128]{2,1,0:T(8,128)S(1)} %get-tuple-element.19), channel_id=1, replica_groups=mesh['x'=4,'y_lo'=2,'z'=8,'y_hi'=4,'core'=2] {'core','y_hi'}, dimensions={0} | all-to-all | bytes 819200 | tf_op jit(solution)/shard_map/all_to_all | solution.py:354
  45.5 0.0 copy-done.1
  45.5 0.0 copy-done.2
  45.5 0.0 copy-done.4
  45.5 1.8 %shard_map.113 = f32[104,1024]{1,0:T(8,128)S(1)} custom-call(f32[8,100,128]{2,1,0:T(8,128)S(1)} %all_to_all.20.grad_ref, bf16[100,1024]{1,0:T(8,128)(2,1)S(1)} %copy-done.2, f32[1,1024]{1,0:T(1,128)S(1)} %bitcast.24, f32[8,128]{1,0:T(8,128)S(1)} %bitcast.27, f32[8,128]{1,0:T(8,128)S(1)} %get-tuple-element.20.loss_ref, bf16[1024,1024]{1,0:T(8,128)(2,1)S(1)} %copy-done.1, ...), custom_call_target="tpu_custom_call" | custom-call | flops 419430400 | bytes 4194304 | tf_op jit(solution)/shard_map/pallas_call | solution.py:240
  47.3 0.0 copy-start
  47.3 2.5 %all-gather = f32[208,1024]{1,0:T(8,128)S(1)} all-gather(f32[104,1024]{1,0:T(8,128)S(1)} %shard_map.113), channel_id=2, replica_groups=mesh['x'=4,'y_lo'=2,'z'=8,'y_hi'=4,'core'=2] {'core'}, dimensions={0}, use_global_device_ids=true | all-gather | bytes 1277952 | tf_op jit(solution)/shard_map/all_gather | solution.py:371
  49.8 0.1 shard_map.114
  50.0 32.1 %all_to_all.21 = f32[256,2,128]{2,1,0:T(2,128)S(1)} all-to-all(f32[256,2,128]{2,1,0:T(2,128)S(1)} %bitcast.21), channel_id=1, replica_groups=mesh['x'=4,'y_lo'=2,'z'=8,'y_hi'=4,'core'=2] {'x','y_hi','y_lo','z'}, dimensions={0} | all-to-all | bytes 524288 | tf_op jit(solution)/shard_map/all_to_all | solution.py:354
  82.1 0.8 shard_map.115
  82.9 10.0 %all-to-all-start.3 = ((f32[256,2,128]{2,1,0:T(2,128)}), f32[256,2,128]{2,1,0:T(2,128)S(1)}, u32[]{:S(2)}, u32[]{:S(2)}) async-start(f32[256,2,128]{2,1,0:T(2,128)} %bitcast.11), calls=%async_computation.3 | async-start | bytes 524288 | tf_op jit(solution)/shard_map/all_to_all | solution.py:354
  92.9 0.0 copy-done
  92.9 3.8 %shard_map.116 = bf16[1024,1024]{1,0:T(8,128)(2,1)} custom-call(bf16[1024,1024]{1,0:T(8,128)(2,1)S(1)} %bitcast.18, f32[8,100,128]{2,1,0:T(8,128)S(1)} %all_to_all.20.grad_ref, bf16[100,1024]{1,0:T(8,128)(2,1)S(1)} %copy-done.2, f32[1,1024]{1,0:T(1,128)S(1)} %bitcast.25, f32[8,128]{1,0:T(8,128)S(1)} %get-tuple-element.23.lat_ref), custom_call_target="tpu_custom_call" | custom-call | flops 209715200 | bytes 12582912 | tf_op jit(solution)/shard_map/pallas_call | solution.py:336
  96.7 8.6 %all-to-all-done.3 = f32[256,2,128]{2,1,0:T(2,128)S(1)} async-done(((f32[256,2,128]{2,1,0:T(2,128)}), f32[256,2,128]{2,1,0:T(2,128)S(1)}, u32[]{:S(2)}, u32[]{:S(2)}) %all-to-all-start.3) | async-done | bytes 262176 | tf_op jit(solution)/shard_map/all_to_all | solution.py:354
  105.3 5.4 %all_gather.11.parts_ref = f32[1024,128]{1,0:T(8,128)S(1)} all-gather(f32[512,128]{1,0:T(8,128)S(1)} %bitcast.30), channel_id=1, replica_groups=mesh['x'=4,'y_lo'=2,'z'=8,'y_hi'=4,'core'=2] {'core'}, dimensions={0}, use_global_device_ids=true | all-gather | bytes 786432 | tf_op jit(solution)/shard_map/all_gather | solution.py:377
  110.7 1.1 shard_map.117
Async XLA Ops:
  4.6 23.7 %all-to-all-start = ((f32[8,100,128]{2,1,0:T(8,128)}), f32[8,100,128]{2,1,0:T(8,128)S(1)}, u32[]{:S(2)}, u32[]{:S(2)}) async-start(f32[8,100,128]{2,1,0:T(8,128)} %get-tuple-element.17), calls=%async_computation | async-start | bytes 851968 | tf_op jit(solution)/shard_map/all_to_all | solution.py:354
  14.9 13.4 %copy-start.3 = (bf16[100,1024]{1,0:T(8,128)(2,1)S(1)}, bf16[100,1024]{1,0:T(8,128)(2,1)}, u32[]{:S(2)}) copy-start(bf16[100,1024]{1,0:T(8,128)(2,1)} %obs_ref.1) | copy-start | bytes 614404
  14.9 13.4 %copy-start.5 = (f32[1024]{0:T(1024)S(1)}, f32[1024]{0:T(1024)}, u32[]{:S(2)}) copy-start(f32[1024]{0:T(1024)} %param.9) | copy-start | bytes 12292
  14.9 13.4 %copy-start.6 = (f32[100]{0:T(128)S(1)}, f32[100]{0:T(128)}, u32[]{:S(2)}) copy-start(f32[100]{0:T(128)} %param.10) | copy-start | bytes 1204
  14.9 30.6 %copy-start.1 = (bf16[1024,1024]{1,0:T(8,128)(2,1)S(1)}, bf16[1024,1024]{1,0:T(8,128)(2,1)}, u32[]{:S(2)}) copy-start(bf16[1024,1024]{1,0:T(8,128)(2,1)} %get-tuple-element.21.normed_ref) | copy-start | bytes 6291460
  14.9 30.6 %copy-start.2 = (bf16[100,1024]{1,0:T(8,128)(2,1)S(1)}, bf16[100,1024]{1,0:T(8,128)(2,1)}, u32[]{:S(2)}) copy-start(bf16[100,1024]{1,0:T(8,128)(2,1)} %weight_ref.3) | copy-start | bytes 614404
  14.9 30.6 %copy-start.4 = (f32[1024]{0:T(1024)S(1)}, f32[1024]{0:T(1024)}, u32[]{:S(2)}) copy-start(f32[1024]{0:T(1024)} %param.13) | copy-start | bytes 12292
  47.3 45.6 %copy-start = (bf16[1,1024,1024]{2,1,0:T(8,128)(2,1)S(1)}, bf16[1,1024,1024]{2,1,0:T(8,128)(2,1)}, u32[]{:S(2)}) copy-start(bf16[1,1024,1024]{2,1,0:T(8,128)(2,1)} %param.7) | copy-start | bytes 6291460
  82.9 22.4 %all-to-all-start.3 = ((f32[256,2,128]{2,1,0:T(2,128)}), f32[256,2,128]{2,1,0:T(2,128)S(1)}, u32[]{:S(2)}, u32[]{:S(2)}) async-start(f32[256,2,128]{2,1,0:T(2,128)} %bitcast.11), calls=%async_computation.3 | async-start | bytes 524288 | tf_op jit(solution)/shard_map/all_to_all | solution.py:354

commit v8 on v7

--- a/solution.py
+++ b/solution.py
@@ -79,9 +79,7 @@
         copy.start()
     for copy in large[1:]:
         copy.start()
-    for copy in small:
-        copy.wait()
-    bias = column(bias_ref[...])[:V]
+    small[0].wait()
     back = []
     for t in range(tiles + 1):
         if t < tiles:
@@ -91,6 +89,10 @@
                 normed_ref[block] = scaled_rows(fields_ref, block, gain_ref[...]).astype(bf16)
             back.append(pltpu.make_async_copy(normed_ref.at[rows[t]], normed_hbm.at[rows[t]], out_sems.at[t, 1]))
             back[-1].start()
+        if t == 1:
+            for copy in small[1:]:
+                copy.wait()
+            bias = column(bias_ref[...])[:V]
         if t > 0:
             done = normed_ref[rows[t - 1]]
             pred = lax.dot_general(weight_ref[...], done, NT, preferred_element_type=f32)

time: 112 us -> 112 us (level)
  no operation moved by 1% of the time
where the time goes in v8:
time: 112 us
  blocking collectives  56.7 us (51%)
  starting transfers between devices  20.3 us (18%)
  waiting for transfers between devices  17.3 us (15%)
  Pallas kernels  16.9 us (15%)
    all_to_all x2, blocking collectives, swap(): return lax.all_to_all(array, axes, split_axis=0, concat_axis=0, tiled=True)  48.8 us
    all_to_all x2, starting transfers between devices, swap(): return lax.all_to_all(array, axes, split_axis=0, concat_axis=0, tiled=True)  20.3 us
    all_to_all x2, waiting for transfers between devices, swap(): return lax.all_to_all(array, axes, split_axis=0, concat_axis=0, tiled=True)  17.3 us
    all_gather x1, blocking collectives, shards(): sums = lax.all_gather(sums.reshape(D // 2, LANES), 'core', tiled=True)  5.39 us
    pallas_call x1, Pallas kernels, residual(): pl.pallas_call(residual_kernel, grid=(LOCAL // TILE,), in_specs=[block, p...  4.66 us
    pallas_call x1, Pallas kernels, forward(): pl.pallas_call(forward_kernel, in_specs=[HBM] * 4, out_specs=[HBM] * 2, o...  4.08 us
    pallas_call x1, Pallas kernels, fields_part(): pl.pallas_call(functools.partial(fields_kernel, points_total), grid=(LOCA...  3.76 us
    all_gather x1, blocking collectives, shards(): sums = lax.all_gather(sums, 'core')  2.55 us
  transfers between devices with their start and end apart: 2, of which 2 were waited for; matrix products, arithmetic and copies ran while one was open for 0% of the time, Pallas kernels for 8%

profile of v8, /device:TPU:1, one launch (start us, length us, event | category | flops | bytes accessed | tf_op | source)
XLA Modules:
  0.0 111.9 jit_solution(5199118723239733815)
XLA Ops:
  0.6 4.1 %shard_map.110 = (f32[8,100,128]{2,1,0:T(8,128)}, bf16[1024,1024]{1,0:T(8,128)(2,1)}) custom-call(bf16[1024,1024]{1,0:T(8,128)(2,1)} %bitcast.16, bf16[100,1024]{1,0:T(8,128)(2,1)} %weight_ref.3, f32[1,100]{1,0:T(1,128)} %bitcast.31, f32[1,1024]{1,0:T(1,128)} %bitcast.22), custom_call_target="tpu_custom_call" | custom-call | flops 209715200 | bytes 3145728 | tf_op jit(solution)/shard_map/pallas_call | solution.py:111
  4.7 10.3 %all-to-all-start = ((f32[8,100,128]{2,1,0:T(8,128)}), f32[8,100,128]{2,1,0:T(8,128)S(1)}, u32[]{:S(2)}, u32[]{:S(2)}) async-start(f32[8,100,128]{2,1,0:T(8,128)} %get-tuple-element.17), calls=%async_computation | async-start | bytes 851968 | tf_op jit(solution)/shard_map/all_to_all | solution.py:356
  15.0 0.0 copy-start.3
  15.0 0.0 copy-start.5
  15.0 0.0 copy-start.6
  15.0 0.0 copy-start.1
  15.0 0.0 copy-start.2
  15.0 0.0 copy-start.4
  15.0 4.7 %shard_map.111.resid_hbm = f8e4m3fn[2048,1024]{1,0:T(32,128)(4,1)} custom-call(bf16[1024,1024]{1,0:T(8,128)(2,1)} %bitcast.17, f32[1,1024]{1,0:T(1,128)} %bitcast.23), custom_call_target="tpu_custom_call" | custom-call | flops 12582912 | bytes 6291456 | tf_op jit(solution)/shard_map/pallas_call | solution.py:144
  19.7 8.7 %all-to-all-done.pred_ref = f32[8,100,128]{2,1,0:T(8,128)S(1)} async-done(((f32[8,100,128]{2,1,0:T(8,128)}), f32[8,100,128]{2,1,0:T(8,128)S(1)}, u32[]{:S(2)}, u32[]{:S(2)}) %all-to-all-start) | async-done | bytes 409632 | tf_op jit(solution)/shard_map/all_to_all | solution.py:356
  28.4 0.0 copy-done.3
  28.4 0.0 copy-done.5
  28.4 0.0 copy-done.6
  28.4 0.6 shard_map.112
  29.0 16.6 %all_to_all.20.grad_ref = f32[8,100,128]{2,1,0:T(8,128)S(1)} all-to-all(f32[8,100,128]{2,1,0:T(8,128)S(1)} %get-tuple-element.19), channel_id=1, replica_groups=mesh['x'=4,'y_lo'=2,'z'=8,'y_hi'=4,'core'=2] {'core','y_hi'}, dimensions={0} | all-to-all | bytes 819200 | tf_op jit(solution)/shard_map/all_to_all | solution.py:356
  45.6 0.0 copy-done.1
  45.6 0.0 copy-done.2
  45.6 0.0 copy-done.4
  45.6 1.8 %shard_map.113 = f32[104,1024]{1,0:T(8,128)S(1)} custom-call(f32[8,100,128]{2,1,0:T(8,128)S(1)} %all_to_all.20.grad_ref, bf16[100,1024]{1,0:T(8,128)(2,1)S(1)} %copy-done.2, f32[1,1024]{1,0:T(1,128)S(1)} %bitcast.24, f32[8,128]{1,0:T(8,128)S(1)} %bitcast.27, f32[8,128]{1,0:T(8,128)S(1)} %get-tuple-element.20.loss_ref, bf16[1024,1024]{1,0:T(8,128)(2,1)S(1)} %copy-done.1, ...), custom_call_target="tpu_custom_call" | custom-call | flops 419430400 | bytes 4194304 | tf_op jit(solution)/shard_map/pallas_call | solution.py:242
  47.4 0.0 copy-start
  47.4 2.5 %all-gather = f32[208,1024]{1,0:T(8,128)S(1)} all-gather(f32[104,1024]{1,0:T(8,128)S(1)} %shard_map.113), channel_id=2, replica_groups=mesh['x'=4,'y_lo'=2,'z'=8,'y_hi'=4,'core'=2] {'core'}, dimensions={0}, use_global_device_ids=true | all-gather | bytes 1277952 | tf_op jit(solution)/shard_map/all_gather | solution.py:373
  50.0 0.1 shard_map.114
  50.1 32.1 %all_to_all.21 = f32[256,2,128]{2,1,0:T(2,128)S(1)} all-to-all(f32[256,2,128]{2,1,0:T(2,128)S(1)} %bitcast.21), channel_id=1, replica_groups=mesh['x'=4,'y_lo'=2,'z'=8,'y_hi'=4,'core'=2] {'x','y_hi','y_lo','z'}, dimensions={0} | all-to-all | bytes 524288 | tf_op jit(solution)/shard_map/all_to_all | solution.py:356
  82.2 0.8 shard_map.115
  83.0 10.0 %all-to-all-start.3 = ((f32[256,2,128]{2,1,0:T(2,128)}), f32[256,2,128]{2,1,0:T(2,128)S(1)}, u32[]{:S(2)}, u32[]{:S(2)}) async-start(f32[256,2,128]{2,1,0:T(2,128)} %bitcast.11), calls=%async_computation.3 | async-start | bytes 524288 | tf_op jit(solution)/shard_map/all_to_all | solution.py:356
  93.0 0.0 copy-done
  93.0 3.8 %shard_map.116 = bf16[1024,1024]{1,0:T(8,128)(2,1)} custom-call(bf16[1024,1024]{1,0:T(8,128)(2,1)S(1)} %bitcast.18, f32[8,100,128]{2,1,0:T(8,128)S(1)} %all_to_all.20.grad_ref, bf16[100,1024]{1,0:T(8,128)(2,1)S(1)} %copy-done.2, f32[1,1024]{1,0:T(1,128)S(1)} %bitcast.25, f32[8,128]{1,0:T(8,128)S(1)} %get-tuple-element.23.lat_ref), custom_call_target="tpu_custom_call" | custom-call | flops 209715200 | bytes 12582912 | tf_op jit(solution)/shard_map/pallas_call | solution.py:338
  96.8 8.6 %all-to-all-done.3 = f32[256,2,128]{2,1,0:T(2,128)S(1)} async-done(((f32[256,2,128]{2,1,0:T(2,128)}), f32[256,2,128]{2,1,0:T(2,128)S(1)}, u32[]{:S(2)}, u32[]{:S(2)}) %all-to-all-start.3) | async-done | bytes 262176 | tf_op jit(solution)/shard_map/all_to_all | solution.py:356
  105.4 5.4 %all_gather.11.parts_ref = f32[1024,128]{1,0:T(8,128)S(1)} all-gather(f32[512,128]{1,0:T(8,128)S(1)} %bitcast.30), channel_id=1, replica_groups=mesh['x'=4,'y_lo'=2,'z'=8,'y_hi'=4,'core'=2] {'core'}, dimensions={0}, use_global_device_ids=true | all-gather | bytes 786432 | tf_op jit(solution)/shard_map/all_gather | solution.py:379
  110.8 1.1 shard_map.117
Async XLA Ops:
  4.7 23.7 %all-to-all-start = ((f32[8,100,128]{2,1,0:T(8,128)}), f32[8,100,128]{2,1,0:T(8,128)S(1)}, u32[]{:S(2)}, u32[]{:S(2)}) async-start(f32[8,100,128]{2,1,0:T(8,128)} %get-tuple-element.17), calls=%async_computation | async-start | bytes 851968 | tf_op jit(solution)/shard_map/all_to_all | solution.py:356
  15.0 13.4 %copy-start.3 = (bf16[100,1024]{1,0:T(8,128)(2,1)S(1)}, bf16[100,1024]{1,0:T(8,128)(2,1)}, u32[]{:S(2)}) copy-start(bf16[100,1024]{1,0:T(8,128)(2,1)} %obs_ref.1) | copy-start | bytes 614404
  15.0 13.4 %copy-start.5 = (f32[1024]{0:T(1024)S(1)}, f32[1024]{0:T(1024)}, u32[]{:S(2)}) copy-start(f32[1024]{0:T(1024)} %param.9) | copy-start | bytes 12292
  15.0 13.4 %copy-start.6 = (f32[100]{0:T(128)S(1)}, f32[100]{0:T(128)}, u32[]{:S(2)}) copy-start(f32[100]{0:T(128)} %param.10) | copy-start | bytes 1204
  15.0 30.6 %copy-start.1 = (bf16[1024,1024]{1,0:T(8,128)(2,1)S(1)}, bf16[1024,1024]{1,0:T(8,128)(2,1)}, u32[]{:S(2)}) copy-start(bf16[1024,1024]{1,0:T(8,128)(2,1)} %get-tuple-element.21.normed_ref) | copy-start | bytes 6291460
  15.0 30.6 %copy-start.2 = (bf16[100,1024]{1,0:T(8,128)(2,1)S(1)}, bf16[100,1024]{1,0:T(8,128)(2,1)}, u32[]{:S(2)}) copy-start(bf16[100,1024]{1,0:T(8,128)(2,1)} %weight_ref.3) | copy-start | bytes 614404
  15.0 30.6 %copy-start.4 = (f32[1024]{0:T(1024)S(1)}, f32[1024]{0:T(1024)}, u32[]{:S(2)}) copy-start(f32[1024]{0:T(1024)} %param.13) | copy-start | bytes 12292
  47.4 45.6 %copy-start = (bf16[1,1024,1024]{2,1,0:T(8,128)(2,1)S(1)}, bf16[1,1024,1024]{2,1,0:T(8,128)(2,1)}, u32[]{:S(2)}) copy-start(bf16[1,1024,1024]{2,1,0:T(8,128)(2,1)} %param.7) | copy-start | bytes 6291460
  83.0 22.4 %all-to-all-start.3 = ((f32[256,2,128]{2,1,0:T(2,128)}), f32[256,2,128]{2,1,0:T(2,128)S(1)}, u32[]{:S(2)}, u32[]{:S(2)}) async-start(f32[256,2,128]{2,1,0:T(2,128)} %bitcast.11), calls=%async_computation.3 | async-start | bytes 524288 | tf_op jit(solution)/shard_map/all_to_all | solution.py:356
